TPU v7x, 256 devices: a whole 4x4x8 slice. The times are simulated.
256 devices in a mesh: dp: 16 (over z, core), tensor: 16 (over x, y).
Axes of the slice: x: 4, y: 4, z: 8, core: 2. Of those that a mesh axis runs over, the one named last changes fastest.
Arguments:
- hidden: bfloat16 [16384, 28672], P('dp', 'tensor'), may hold values from -6 to 6
- output_gradient: bfloat16 [16384, 8192], P('dp', 'tensor'), may hold values from -1.5 to 1.5
- block_adapter_index: int32 [128], P('dp'), may hold values from 0 to 511, as said below
- adapter_down_factors: bfloat16 [512, 16, 28672], P('dp', None, 'tensor'), may hold values from -0.03125 to 0.03125
- adapter_up_factors: bfloat16 [512, 16, 8192], P('dp', None, 'tensor'), may hold values from -0.0625 to 0.0625
Outputs:
- grad_hidden: bfloat16 [16384, 28672], P('dp', 'tensor')
- grad_a: bfloat16 [512, 16, 28672], P('dp', None, 'tensor')
- grad_b: bfloat16 [512, 16, 8192], P('dp', None, 'tensor')
Inputs may be any that keep to these rules, and one draw needn't show every extreme that they name: `block_adapter_index`: adapter a belongs to owner a // 32. Among the 8 blocks of one index of dp at most 2 take adapters of one owner, and on every index some owner is taken by exactly 2 blocks.
All inputs are finite; a program needn't handle non-finite values.
Results may differ from a plain program's by a relative error of at most 0.0053.
Values may be sent and summed in bfloat16 or wider, within the bound.
A program may use at most 64 MiB of HBM per device.

v0:
```python
import jax
import jax.numpy as jnp
from jax import lax
from jax.sharding import PartitionSpec as P

ADAPTER_RANK = 16
BLOCK = 128
CAP = 2


adapter_scale = 2.0


def shards(hidden, output_gradient, block_adapter_index, adapter_down_factors, adapter_up_factors):
    dp_size = lax.axis_size("dp")
    my_index = lax.axis_index("dp")
    block_count = block_adapter_index.shape[0]
    owned_adapter_count = adapter_down_factors.shape[0]
    ff_local = hidden.shape[1]
    d_local = output_gradient.shape[1]
    slot_count = dp_size * CAP
    all_ids = lax.all_gather(block_adapter_index, "dp", axis=0, tiled=True).reshape(
        dp_size, block_count
    )
    owners = all_ids // owned_adapter_count
    local_ids = all_ids % owned_adapter_count
    same_owner = owners[:, :, None] == owners[:, None, :]
    block_range = jnp.arange(block_count, dtype=jnp.int32)
    earlier = block_range[None, :] < block_range[:, None]
    rank_in = jnp.sum(jnp.logical_and(same_owner, earlier[None, :, :]), axis=2)
    cap_range = jnp.arange(CAP, dtype=jnp.int32)
    chosen = jnp.logical_and(
        (owners == my_index)[:, None, :], rank_in[:, None, :] == cap_range[None, :, None]
    )
    owned_range = jnp.arange(owned_adapter_count, dtype=jnp.int32)
    local_match = local_ids[:, :, None] == owned_range[None, None, :]
    selection_table = jnp.sum(
        jnp.logical_and(chosen[:, :, :, None], local_match[:, None, :, :]), axis=2
    )
    selection_table = selection_table.reshape(slot_count, owned_adapter_count).astype(jnp.bfloat16)
    send_a = jnp.einsum(
        "dz,zeg->deg", selection_table, adapter_down_factors, preferred_element_type=jnp.float32
    ).astype(jnp.bfloat16)
    send_b = jnp.einsum(
        "ge,elq->glq", selection_table, adapter_up_factors, preferred_element_type=jnp.float32
    ).astype(jnp.bfloat16)
    send_a = send_a.reshape(dp_size, CAP, ADAPTER_RANK, ff_local)
    send_b = send_b.reshape(dp_size, CAP, ADAPTER_RANK, d_local)
    fetched_a, fetched_b = (
        lax.all_to_all(send_a, "dp", split_axis=0, concat_axis=0, tiled=True),
        lax.all_to_all(send_b, "dp", split_axis=0, concat_axis=0, tiled=True),
    )
    fetched_a = fetched_a.reshape(slot_count, ADAPTER_RANK, ff_local)
    fetched_b = fetched_b.reshape(slot_count, ADAPTER_RANK, d_local)
    my_owners = jnp.take(owners, my_index, axis=0)
    my_ranks = jnp.take(rank_in, my_index, axis=0)
    my_slots = my_owners * CAP + my_ranks
    down_factor = jnp.take(fetched_a, my_slots, axis=0)
    up_factor = jnp.take(fetched_b, my_slots, axis=0)
    hid_blocks = hidden.reshape(block_count, BLOCK, ff_local)
    out_blocks = output_gradient.reshape(block_count, BLOCK, d_local)
    proj_part = jnp.einsum(
        "jtf,jrf->jtr", hid_blocks, down_factor, preferred_element_type=jnp.float32
    )
    back_part = jnp.einsum(
        "jtd,jrd->jtr", out_blocks, up_factor, preferred_element_type=jnp.float32
    )
    proj, back = lax.psum((proj_part, back_part), "tensor")
    projected_up = proj.astype(jnp.bfloat16)
    backward_up = back.astype(jnp.bfloat16)
    block_down_gradient = (
        adapter_scale
        * jnp.einsum("jtr,jtf->jrf", backward_up, hid_blocks, preferred_element_type=jnp.float32)
    ).astype(jnp.bfloat16)
    block_up_gradient = (
        adapter_scale
        * jnp.einsum("jtr,jtd->jrd", projected_up, out_blocks, preferred_element_type=jnp.float32)
    ).astype(jnp.bfloat16)
    gradient_rows = adapter_scale * jnp.einsum(
        "jtr,jrf->jtf", backward_up, down_factor, preferred_element_type=jnp.float32
    )
    grad_hidden = gradient_rows.astype(jnp.bfloat16).reshape(block_count * BLOCK, ff_local)
    slot_range = jnp.arange(slot_count, dtype=jnp.int32)
    place_table = (slot_range[:, None] == my_slots[None, :]).astype(jnp.bfloat16)
    back_a = jnp.einsum(
        "kj,jrf->krf", place_table, block_down_gradient, preferred_element_type=jnp.float32
    ).astype(jnp.bfloat16)
    back_bb = jnp.einsum(
        "kj,jrd->krd", place_table, block_up_gradient, preferred_element_type=jnp.float32
    ).astype(jnp.bfloat16)
    back_a = back_a.reshape(dp_size, CAP, ADAPTER_RANK, ff_local)
    back_bb = back_bb.reshape(dp_size, CAP, ADAPTER_RANK, d_local)
    recv_a, recv_b = (
        lax.all_to_all(back_a, "dp", split_axis=0, concat_axis=0, tiled=True),
        lax.all_to_all(back_bb, "dp", split_axis=0, concat_axis=0, tiled=True),
    )
    sum_table = jnp.transpose(selection_table)
    grad_a = jnp.einsum(
        "ak,krf->arf",
        sum_table,
        recv_a.reshape(slot_count, ADAPTER_RANK, ff_local),
        preferred_element_type=jnp.float32,
    )
    grad_b = jnp.einsum(
        "ak,krd->ard",
        sum_table,
        recv_b.reshape(slot_count, ADAPTER_RANK, d_local),
        preferred_element_type=jnp.float32,
    )
    return (grad_hidden, grad_a.astype(jnp.bfloat16), grad_b.astype(jnp.bfloat16))


def solution(mesh):
    placed = (
        P("dp", "tensor"),
        P("dp", "tensor"),
        P("dp"),
        P("dp", None, "tensor"),
        P("dp", None, "tensor"),
    )
    return jax.shard_map(
        shards,
        mesh=mesh,
        in_specs=placed,
        out_specs=(P("dp", "tensor"), P("dp", None, "tensor"), P("dp", None, "tensor")),
        check_vma=False,
    )
```

profile of v0, /device:TPU:1, one launch (start us, length us, event | category | flops | bytes accessed | tf_op | source)
XLA Modules:
  0.0 252.8 jit_solution(16364598477550580204)
XLA Ops:
  0.6 0.0 copy-start
  0.7 1.4 dynamic-slice.5
  2.7 0.9 dynamic-update-slice.1
  3.6 14.7 %all-reduce = s32[128]{0:T(128)S(1)} all-reduce(s32[128]{0:T(128)S(1)} %dynamic-update-slice.1), channel_id=1, replica_groups=mesh['dp'=16,'tensor'=16] {'dp'}, use_global_device_ids=true, to_apply=%add | all-reduce | flops 128 | bytes 1024
  18.3 0.1 reshape.156
  18.4 0.1 copy.59
  18.5 0.1 convert_reduce_fusion.1
  18.6 0.1 copy.61
  18.6 0.1 iota_compare_fusion
  18.8 0.1 convert_reduce_fusion
  18.9 1.5 convolution_convert_fusion.2
  20.4 0.2 reshape.157
  20.6 1.3 copy.63
  21.9 6.5 %all-to-all-start = ((bf16[16,2,16,512]{3,1,2,0:T(2,128)(2,1)}), bf16[16,2,16,512]{3,1,2,0:T(2,128)(2,1)S(1)}, u32[]{:S(2)}, u32[]{:S(2)}) async-start(bf16[16,2,16,512]{3,1,2,0:T(2,128)(2,1)} %copy.63), calls=%async_computation | async-start | bytes 1048576 | tf_op jit(solution)/shard_map/all_to_all | solution.py:51
  28.4 0.0 copy-done
  28.4 2.4 convolution_convert_fusion.1
  30.8 4.8 %reshape.160 = bf16[16,2,16,1792]{3,1,0,2:T(2,128)(2,1)} reshape(bf16[32,16,1792]{2,0,1:T(8,128)(2,1)} %convolution_convert_fusion.1) | data formatting | bytes 3670016 | tf_op jit(solution)/shard_map/reshape | solution.py:47
  35.6 4.4 %copy.66 = bf16[16,2,16,1792]{3,1,2,0:T(2,128)(2,1)} copy(bf16[16,2,16,1792]{3,1,0,2:T(2,128)(2,1)} %reshape.160) | data formatting | bytes 3670016 | tf_op jit(solution)/shard_map/reshape | solution.py:47
  40.0 0.0 copy-start.1
  40.0 5.8 %all-to-all-done = bf16[16,2,16,512]{3,1,2,0:T(2,128)(2,1)S(1)} async-done(((bf16[16,2,16,512]{3,1,2,0:T(2,128)(2,1)}), bf16[16,2,16,512]{3,1,2,0:T(2,128)(2,1)S(1)}, u32[]{:S(2)}, u32[]{:S(2)}) %all-to-all-start) | async-done | bytes 524320 | tf_op jit(solution)/shard_map/all_to_all | solution.py:51
  45.7 4.3 %all-to-all-start.1 = ((bf16[16,2,16,1792]{3,1,2,0:T(2,128)(2,1)}), bf16[16,2,16,1792]{3,1,2,0:T(2,128)(2,1)}, u32[]{:S(2)}, u32[]{:S(2)}) async-start(bf16[16,2,16,1792]{3,1,2,0:T(2,128)(2,1)} %copy.66), calls=%async_computation.1 | async-start | bytes 3670016 | tf_op jit(solution)/shard_map/all_to_all | solution.py:50
  50.1 0.2 select_reduce_fusion
  50.3 0.9 copy.64
  51.2 1.6 gather_fusion
  52.8 0.0 copy-done.1
  52.8 0.4 convolution_bitcast_fusion.2
  53.2 39.2 %all-to-all-done.1 = bf16[16,2,16,1792]{3,1,2,0:T(2,128)(2,1)} async-done(((bf16[16,2,16,1792]{3,1,2,0:T(2,128)(2,1)}), bf16[16,2,16,1792]{3,1,2,0:T(2,128)(2,1)}, u32[]{:S(2)}, u32[]{:S(2)}) %all-to-all-start.1) | async-done | bytes 1835040 | tf_op jit(solution)/shard_map/all_to_all | solution.py:50
  92.4 3.0 %copy.67 = bf16[16,2,16,1792]{3,2,1,0:T(8,128)(2,1)} copy(bf16[16,2,16,1792]{3,1,2,0:T(2,128)(2,1)} %all-to-all-done.1) | data formatting | bytes 3670016 | tf_op jit(solution)/shard_map/all_to_all | solution.py:50
  95.4 2.1 gather_fusion.1
  97.5 3.1 %convolution_bitcast_fusion.1 = f32[8,128,16]{1,2,0:T(8,128)S(1)} fusion(bf16[8,128,1792]{2,1,0:T(8,128)(2,1)} %bitcast.55, bf16[8,16,1792]{2,1,0:T(8,128)(2,1)S(1)} %gather_fusion.1, pred[8]{0:T(512)(128)(4,1)S(1)} %get-tuple-element.32), kind=kOutput, calls=%fused_computation.16 | convolution fusion | flops 58949632 | bytes 4194312 | tf_op jit(solution)/shard_map/jtf,jrf->jtr/dot_general | solution.py:62
  100.6 61.4 %all-reduce.3 = (bf16[8,128,16]{1,2,0:T(8,128)(2,1)S(1)}, bf16[8,128,16]{1,2,0:T(8,128)(2,1)S(1)}) all-reduce(f32[8,128,16]{1,2,0:T(8,128)S(1)} %convolution_bitcast_fusion.2, f32[8,128,16]{1,2,0:T(8,128)S(1)} %convolution_bitcast_fusion.1), channel_id=1, replica_groups=mesh['dp'=16,'tensor'=16] {'tensor'}, use_global_device_ids=true, to_apply=%region_2.4 | all-reduce | flops 32768 | bytes 196608 | tf_op jit(solution)/shard_map/psum | solution.py:68
  162.0 0.2 fusion.4
  162.3 0.4 convolution_convert_fusion.3
  162.7 0.2 reshape.165
  162.9 1.3 copy.73
  164.2 18.8 %all-to-all-start.3 = ((bf16[16,2,16,512]{3,1,2,0:T(2,128)(2,1)}), bf16[16,2,16,512]{3,1,2,0:T(2,128)(2,1)S(1)}, u32[]{:S(2)}, u32[]{:S(2)}) async-start(bf16[16,2,16,512]{3,1,2,0:T(2,128)(2,1)} %copy.73), calls=%async_computation.3 | async-start | bytes 1048576 | tf_op jit(solution)/shard_map/all_to_all | solution.py:95
  183.0 2.6 %fusion = bf16[8,16,1792]{2,1,0:T(8,128)(2,1)S(1)} fusion(bf16[8,128,1792]{2,1,0:T(8,128)(2,1)} %bitcast.56, bf16[8,128,16]{1,2,0:T(8,128)(2,1)S(1)} %get-tuple-element.30), kind=kOutput, calls=%fused_computation.7 | convolution fusion | flops 59179008 | bytes 4161536 | tf_op jit(solution)/shard_map/jtr,jtf->jrf/dot_general | solution.py:73
  185.7 2.0 convolution_convert_fusion
  187.7 4.8 %reshape.164 = bf16[16,2,16,1792]{3,1,0,2:T(2,128)(2,1)} reshape(bf16[32,16,1792]{2,0,1:T(8,128)(2,1)} %convolution_convert_fusion) | data formatting | bytes 3670016 | tf_op jit(solution)/shard_map/reshape | solution.py:91
  192.4 4.4 %copy.69 = bf16[16,2,16,1792]{3,1,2,0:T(2,128)(2,1)} copy(bf16[16,2,16,1792]{3,1,0,2:T(2,128)(2,1)} %reshape.164) | data formatting | bytes 3670016 | tf_op jit(solution)/shard_map/reshape | solution.py:91
  196.8 3.5 %all-to-all-done.3 = bf16[16,2,16,512]{3,1,2,0:T(2,128)(2,1)S(1)} async-done(((bf16[16,2,16,512]{3,1,2,0:T(2,128)(2,1)}), bf16[16,2,16,512]{3,1,2,0:T(2,128)(2,1)S(1)}, u32[]{:S(2)}, u32[]{:S(2)}) %all-to-all-start.3) | async-done | bytes 524320 | tf_op jit(solution)/shard_map/all_to_all | solution.py:95
  200.4 4.3 %all-to-all-start.2 = ((bf16[16,2,16,1792]{3,1,2,0:T(2,128)(2,1)}), bf16[16,2,16,1792]{3,1,2,0:T(2,128)(2,1)}, u32[]{:S(2)}, u32[]{:S(2)}) async-start(bf16[16,2,16,1792]{3,1,2,0:T(2,128)(2,1)} %copy.69), calls=%async_computation.2 | async-start | bytes 3670016 | tf_op jit(solution)/shard_map/all_to_all | solution.py:94
  204.7 3.0 %multiply_convert_fusion = bf16[8,128,1792]{2,1,0:T(8,128)(2,1)} fusion(bf16[8,16,1792]{2,1,0:T(8,128)(2,1)S(1)} %gather_fusion.1, pred[8]{0:T(512)(128)(4,1)S(1)} %get-tuple-element.32, bf16[8,128,16]{1,2,0:T(8,128)(2,1)S(1)} %get-tuple-element.30), kind=kOutput, calls=%fused_computation.2 | convolution fusion | flops 62619648 | bytes 4161544 | tf_op jit(solution)/shard_map/jtr,jrf->jtf/dot_general | solution.py:79
  207.7 0.4 fusion.3
  208.1 1.1 copy.77
  209.2 38.6 %all-to-all-done.2 = bf16[16,2,16,1792]{3,1,2,0:T(2,128)(2,1)} async-done(((bf16[16,2,16,1792]{3,1,2,0:T(2,128)(2,1)}), bf16[16,2,16,1792]{3,1,2,0:T(2,128)(2,1)}, u32[]{:S(2)}, u32[]{:S(2)}) %all-to-all-start.2) | async-done | bytes 1835040 | tf_op jit(solution)/shard_map/all_to_all | solution.py:94
  247.8 2.7 %bitcast_convert_fusion = bf16[32,16,1792]{2,0,1:T(8,128)(2,1)S(1)} fusion(bf16[16,2,16,1792]{3,1,2,0:T(2,128)(2,1)} %all-to-all-done.2, bf16[16,2,32]{2,1,0:T(2,128)(2,1)S(1)} %convert_element_type.50), kind=kOutput, calls=%fused_computation.3 | convolution fusion | flops 59637760 | bytes 3672064 | tf_op jit(solution)/shard_map/ak,krf->arf/dot_general | solution.py:98
  250.5 2.2 copy.76
  (9 shorter events, 0.1 us)
Async XLA Ops:
  0.6 27.8 %copy-start = (bf16[32,16,1792]{2,1,0:T(8,128)(2,1)S(1)}, bf16[32,16,1792]{2,1,0:T(8,128)(2,1)}, u32[]{:S(2)}) copy-start(bf16[32,16,1792]{2,1,0:T(8,128)(2,1)} %param.10) | copy-start | bytes 5505028
  21.9 23.8 %all-to-all-start = ((bf16[16,2,16,512]{3,1,2,0:T(2,128)(2,1)}), bf16[16,2,16,512]{3,1,2,0:T(2,128)(2,1)S(1)}, u32[]{:S(2)}, u32[]{:S(2)}) async-start(bf16[16,2,16,512]{3,1,2,0:T(2,128)(2,1)} %copy.63), calls=%async_computation | async-start | bytes 1048576 | tf_op jit(solution)/shard_map/all_to_all | solution.py:51
  40.0 12.8 %copy-start.1 = (bf16[1024,512]{1,0:T(8,128)(2,1)S(1)}, bf16[1024,512]{1,0:T(8,128)(2,1)}, u32[]{:S(2)}) copy-start(bf16[1024,512]{1,0:T(8,128)(2,1)} %param.8) | copy-start | bytes 3145732
  45.7 46.7 %all-to-all-start.1 = ((bf16[16,2,16,1792]{3,1,2,0:T(2,128)(2,1)}), bf16[16,2,16,1792]{3,1,2,0:T(2,128)(2,1)}, u32[]{:S(2)}, u32[]{:S(2)}) async-start(bf16[16,2,16,1792]{3,1,2,0:T(2,128)(2,1)} %copy.66), calls=%async_computation.1 | async-start | bytes 3670016 | tf_op jit(solution)/shard_map/all_to_all | solution.py:50
  164.2 36.1 %all-to-all-start.3 = ((bf16[16,2,16,512]{3,1,2,0:T(2,128)(2,1)}), bf16[16,2,16,512]{3,1,2,0:T(2,128)(2,1)S(1)}, u32[]{:S(2)}, u32[]{:S(2)}) async-start(bf16[16,2,16,512]{3,1,2,0:T(2,128)(2,1)} %copy.73), calls=%async_computation.3 | async-start | bytes 1048576 | tf_op jit(solution)/shard_map/all_to_all | solution.py:95
  200.4 47.5 %all-to-all-start.2 = ((bf16[16,2,16,1792]{3,1,2,0:T(2,128)(2,1)}), bf16[16,2,16,1792]{3,1,2,0:T(2,128)(2,1)}, u32[]{:S(2)}, u32[]{:S(2)}) async-start(bf16[16,2,16,1792]{3,1,2,0:T(2,128)(2,1)} %copy.69), calls=%async_computation.2 | async-start | bytes 3670016 | tf_op jit(solution)/shard_map/all_to_all | solution.py:94
where the time goes:
time: 254 us; the launch traced here: 253 us
  waiting for transfers between devices  87.1 us (34%)
  blocking collectives  76.1 us (30%)
  local copies, waits for them, and re-layouts  34.7 us (14%)
  starting transfers between devices  33.9 us (13%)
  matrix products  18.9 us (7%)
    psum x1, blocking collectives, shards(): proj, back = lax.psum((proj_part, back_part), 'tensor')  61.4 us
    all_to_all x1, waiting for transfers between devices, shards(): lax.all_to_all(send_a, 'dp', split_axis=0, concat_axis=0, tiled=True)  39.2 us
    all_to_all x1, waiting for transfers between devices, shards(): lax.all_to_all(back_a, 'dp', split_axis=0, concat_axis=0, tiled=True)  38.6 us
    all_to_all x1, starting transfers between devices, shards(): lax.all_to_all(back_bb, 'dp', split_axis=0, concat_axis=0, tiled=True)  18.8 us
    unnamed x1, blocking collectives  14.7 us
    reshape x2, local copies, waits for them, and re-layouts, shards(): send_a = send_a.reshape(dp_size, CAP, ADAPTER_RANK, ff_local)  9.19 us
    reshape x2, local copies, waits for them, and re-layouts, shards(): back_a = back_a.reshape(dp_size, CAP, ADAPTER_RANK, ff_local)  9.19 us
    all_to_all x1, starting transfers between devices, shards(): lax.all_to_all(send_b, 'dp', split_axis=0, concat_axis=0, tiled=True)  6.45 us
  transfers between devices with their start and end apart: 4, of which 4 were waited for; matrix products, arithmetic and copies ran while one was open for 13% of the time, Pallas kernels for 0%

commit v1 on v0

--- a/solution.py
+++ b/solution.py
@@ -1,17 +1,32 @@
+import functools
+
 import jax
 import jax.numpy as jnp
 from jax import lax
+from jax.experimental import pallas as pl
+from jax.experimental.pallas import tpu as pltpu
 from jax.sharding import PartitionSpec as P
 
 ADAPTER_RANK = 16
 BLOCK = 128
 CAP = 2
+MESH = pl.DeviceIdType.MESH
+NDP = 16
+NCHIP = 8
+NT = 16
+NBLK = 8
+OWNED = 32
+SLOTS = 28
+GROUP = 4
+CHUNKS = SLOTS // GROUP
+NFIN = 2 * SLOTS + 16
+VMEM_LIMIT = 56 * 1024 * 1024
 
 
 adapter_scale = 2.0
 
 
-def shards(hidden, output_gradient, block_adapter_index, adapter_down_factors, adapter_up_factors):
+def general(hidden, output_gradient, block_adapter_index, adapter_down_factors, adapter_up_factors):
     dp_size = lax.axis_size("dp")
     my_index = lax.axis_index("dp")
     block_count = block_adapter_index.shape[0]
@@ -110,6 +125,450 @@
     return (grad_hidden, grad_a.astype(jnp.bfloat16), grad_b.astype(jnp.bfloat16))
 
 
+def bcast(x, shape=(8, 128)):
+    return jnp.broadcast_to(x, shape)
+
+
+def pick_row(x, sub, row):
+    return bcast(jnp.sum(jnp.where(sub == row, x, 0), axis=0, keepdims=True))
+
+
+def slot_plan(src, dst, own_index, chip, sub, lane):
+    ahead = (dst - src) & 7
+    tie = lane & 1
+    plus = jnp.logical_and(ahead > 0, jnp.logical_or(ahead < 4, jnp.logical_and(ahead == 4, tie == 0)))
+    minus = jnp.logical_or(ahead > 4, jnp.logical_and(ahead == 4, tie == 1))
+    dist = jnp.where(plus, ahead, jnp.where(minus, 8 - ahead, 0))
+    group = jnp.where(ahead > 0, src * 2 + jnp.where(minus, 1, 0), 16)
+    order = group * 1024 + (4 - dist) * 128 + lane
+    row = jnp.concatenate([order] * 16, axis=0)
+    col = jnp.transpose(row)
+    before = jnp.logical_and((row >> 10) == (col >> 10), col < row)
+    rank = bcast(jnp.sum(jnp.where(before, 1, 0), axis=0, keepdims=True))
+    result = []
+    longest = jnp.zeros((8, 128), jnp.int32)
+    for sign, act in ((1, plus), (-1, minus)):
+        def shifted(x, by):
+            by = (sign * by) % 8
+            return pltpu.roll(x, by, 0) if by else x
+
+        counts = [
+            bcast(
+                jnp.sum(
+                    jnp.where(jnp.logical_and(jnp.logical_and(src == sub, act), dist > h), 1, 0),
+                    axis=1,
+                    keepdims=True,
+                )
+            )
+            for h in range(4)
+        ]
+        starts = [jnp.zeros((8, 128), jnp.int32)]
+        for h in range(1, 4):
+            starts.append(
+                jnp.maximum(
+                    starts[h - 1] + shifted(counts[h - 1], h - 1),
+                    shifted(starts[h - 1], 1) + GROUP,
+                )
+            )
+        for h in range(4):
+            here = shifted(counts[h], h)
+            longest = jnp.maximum(longest, jnp.where(here > 0, starts[h] + here, 0))
+        age = (sign * (chip - src)) & 7
+        out_start = jnp.zeros((8, 128), jnp.int32)
+        in_start = jnp.zeros((8, 128), jnp.int32)
+        before_chip = (chip - sign) & 7
+        for h in range(4):
+            out_start = jnp.where(age == h, pick_row(starts[h], sub, chip), out_start)
+            in_start = jnp.where(age == h + 1, pick_row(starts[h], sub, before_chip), in_start)
+        leaves = jnp.logical_and(act, age < dist)
+        arrives = jnp.logical_and(act, age == dist)
+        out_slot = out_start + rank
+        in_slot = in_start + rank
+        source = jnp.where(age == 0, own_index + 1, 65 + in_slot)
+        result.append((leaves, out_slot, source, arrives, in_slot))
+    return result, longest
+
+
+def by_row(mask, place, value, rows):
+    reps = rows // 8
+    wide = [jnp.concatenate([v] * reps, axis=0) for v in (jnp.where(mask, place, -1), value)]
+    sub = lax.broadcasted_iota(jnp.int32, (rows, 128), 0)
+    return jnp.sum(jnp.where(wide[0] == sub, wide[1], 0), axis=1, keepdims=True)
+
+
+def make_tables(ids, me):
+    chip = me // 2
+    sub = lax.broadcasted_iota(jnp.int32, (8, 128), 0)
+    lane = lax.broadcasted_iota(jnp.int32, (8, 128), 1)
+    token_chip = lane >> 4
+    owner_chip = ids >> 6
+    chip_slot = ids & 63
+    mine = (ids >> 5) == me
+    row = (ids & 31) + 1
+    fetch, longest_f = slot_plan(owner_chip, token_chip, chip_slot, chip, sub, lane)
+    back, longest_b = slot_plan(token_chip, owner_chip, lane & 15, chip, sub, lane)
+    fits = jnp.max(jnp.maximum(longest_f, longest_b), axis=0, keepdims=True) <= SLOTS
+    columns = []
+    for plan in (fetch, back):
+        for leaves, out_slot, source, _, _ in plan:
+            columns.append(by_row(leaves, out_slot, source, 32))
+    where = jnp.where(owner_chip == token_chip, chip_slot + 1, 0)
+    for d in range(2):
+        where = jnp.where(fetch[d][3], 65 + d * SLOTS + fetch[d][4], where)
+    columns.append(by_row((lane >> 3) == me, lane & 7, where, 32))
+    for d in range(2):
+        columns.append(by_row(jnp.logical_and(back[d][3], mine), back[d][4], row, 32))
+    stays = jnp.logical_and(jnp.logical_and(owner_chip == token_chip, token_chip == chip), mine)
+    columns.append(by_row(stays, lane & 15, row, 32))
+    wide_lane = lax.broadcasted_iota(jnp.int32, (32, 128), 1)
+    table = jnp.where(jnp.broadcast_to(fits, (32, 128)), 1, 0)
+    for i, column in enumerate(columns):
+        table = jnp.where(wide_lane == i, jnp.broadcast_to(column, (32, 128)), table)
+    return table
+
+
+def wait_bytes(ref, sem):
+    pltpu.make_async_copy(ref, ref, sem).wait()
+
+
+def ring_kernel(hw, dw, ids_ref, hid_hbm, og_hbm, a_hbm, b_hbm, table_ref, fac, pb, fin,
+                idbuf, table, own_r, own_s, picked, stage, hid, og, part, parts, grads, items, arrivals,
+                loc, ids_sem, sib, ring_send, ring_recv, fwd, psum_sem):
+    half = hw + dw
+    pieces = ((0, 640), (640, half - 640))
+    me = lax.axis_index("dp")
+    t = lax.axis_index("tensor")
+    chip = me // 2
+    core = me % 2
+    other = 1 - core
+    sibling = {"dp": chip * 2 + other}
+    ko = pl.multiple_of(core * half, 128)
+    so = pl.multiple_of(other * half, 128)
+    mine32 = pl.ds(pl.multiple_of(core * OWNED, OWNED), OWNED)
+    mine8 = pl.ds(pl.multiple_of(core * NBLK, NBLK), NBLK)
+
+    def far(src, dst, send, recv, where):
+        return pltpu.make_async_remote_copy(
+            src_ref=src, dst_ref=dst, send_sem=send, recv_sem=recv, device_id=where, device_id_type=MESH
+        )
+
+    def cut(ref, width, which):
+        return ref.at[:, :, pl.ds(pl.multiple_of(which * width, 128), width)]
+
+    for ref, dst, width, at in ((a_hbm, own_r, hw, 0), (b_hbm, own_r, dw, hw)):
+        pltpu.make_async_copy(cut(ref, width, core), dst.at[mine32, :, pl.ds(at, width)], loc.at[0]).start()
+    for ref, dst, width, at in ((a_hbm, own_s, hw, 0), (b_hbm, own_s, dw, hw)):
+        pltpu.make_async_copy(cut(ref, width, other), dst.at[mine32, :, pl.ds(at, width)], loc.at[1]).start()
+    pltpu.make_async_copy(hid_hbm, hid, loc.at[2]).start()
+    pltpu.make_async_copy(og_hbm, og, loc.at[3]).start()
+
+    barrier = pltpu.get_barrier_semaphore()
+    for o in range(1, NDP):
+        pl.semaphore_signal(barrier, inc=1, device_id={"dp": lax.rem(me + o, NDP)}, device_id_type=MESH)
+    for o in range(1, NT):
+        pl.semaphore_signal(barrier, inc=1, device_id={"tensor": lax.rem(t + o, NT)}, device_id_type=MESH)
+    lane = lax.broadcasted_iota(jnp.int32, (8, 128), 1)
+    idbuf[me] = jnp.where((lane >> 3) == me, ids_ref[...], 0)
+    pl.semaphore_wait(barrier, NDP - 1 + NT - 1)
+
+    for o in range(1, NDP):
+        far(idbuf.at[me], idbuf.at[me], ids_sem.at[0], ids_sem.at[1], {"dp": lax.rem(me + o, NDP)}).start()
+    for ref, width, at in ((a_hbm, hw, 0), (b_hbm, dw, hw)):
+        far(cut(ref, width, other), own_r.at[mine32, :, pl.ds(at, width)], sib.at[0], sib.at[1], sibling).start()
+    for ref, width, at in ((a_hbm, hw, 0), (b_hbm, dw, hw)):
+        far(cut(ref, width, core), own_s.at[mine32, :, pl.ds(at, width)], sib.at[2], sib.at[3], sibling).start()
+
+    wait_bytes(idbuf.at[pl.ds(0, NDP - 1)], ids_sem.at[1])
+    ids = idbuf[0]
+    for i in range(1, NDP):
+        ids = ids + idbuf[i]
+    table_ref[...] = make_tables(ids, me)
+    to_smem = pltpu.make_async_copy(table_ref, table, loc.at[4])
+    to_smem.start()
+    to_smem.wait()
+
+    def ring(phase, own, count, land):
+        def chunk(d, q, p):
+            return arrivals[((phase * 2 + d) * CHUNKS + q) * 2 + p]
+
+        def copy(d, q, p):
+            at, width = pieces[p]
+            return far(
+                stage.at[phase, d, pl.ds(q * GROUP, GROUP), :, pl.ds(at, width)],
+                chunk(d, q, p),
+                ring_send.at[phase],
+                ring_recv.at[phase, d, q, p],
+                {"dp": lax.rem(chip + (1 if d == 0 else NCHIP - 1), NCHIP) * 2 + core},
+            )
+
+        def landed(d, q, p):
+            at, width = pieces[p]
+            copy(d, q, p).wait_recv()
+            there = land.at[
+                pl.ds(d * SLOTS + q * GROUP, GROUP), :, pl.ds(pl.multiple_of(ko + at, 128), width)
+            ]
+            pltpu.make_async_copy(chunk(d, q, p), there, fwd.at[phase, 0]).start()
+            far(chunk(d, q, p), there, fwd.at[phase, 1], fwd.at[phase, 2], sibling).start()
+
+        for m in range(CHUNKS):
+            for p in range(2):
+                at, width = pieces[p]
+                for d in range(2):
+                    if m > 0:
+                        landed(d, m - 1, p)
+                    for i in range(GROUP):
+                        code = table[m * GROUP + i, phase * 2 + d]
+                        value = own[jnp.clip(code - 1, 0, count - 1), :, pl.ds(at, width)]
+                        for q in range(m):
+                            place = code - 65 - q * GROUP
+                            inside = jnp.logical_and(place >= 0, place < GROUP)
+                            value = jnp.where(inside, chunk(d, q, p)[jnp.clip(place, 0, GROUP - 1)], value)
+                        stage[phase, d, m * GROUP + i, :, pl.ds(at, width)] = value
+                    copy(d, m, p).start()
+        for p in range(2):
+            for d in range(2):
+                landed(d, CHUNKS - 1, p)
+        everything = land.at[pl.ds(0, 2 * SLOTS), :, pl.ds(0, half)]
+        wait_bytes(everything, fwd.at[phase, 0])
+        wait_bytes(everything, fwd.at[phase, 2])
+
+    wait_bytes(own_r.at[pl.ds(0, OWNED)], loc.at[0])
+    wait_bytes(own_r.at[pl.ds(0, OWNED)], sib.at[1])
+    ring(0, own_r, 2 * OWNED, picked)
+    wait_bytes(own_s.at[pl.ds(0, OWNED)], loc.at[1])
+    wait_bytes(own_s.at[pl.ds(0, OWNED)], sib.at[3])
+
+    for j in range(NBLK):
+        code = table[j, 4]
+        near = code <= 64
+        at = jnp.clip(code - 1, 0, 2 * OWNED - 1)
+        away = jnp.clip(code - 65, 0, 2 * SLOTS - 1)
+        for own, o in ((own_r, ko), (own_s, so)):
+            fac[j, :, pl.ds(o, half)] = jnp.where(near, own[at], picked[away, :, pl.ds(o, half)])
+
+    wait_bytes(hid, loc.at[2])
+    wait_bytes(og, loc.at[3])
+    for j in range(NBLK):
+        rows = pl.ds(j * BLOCK, BLOCK)
+        for i, ref, base, width in ((j, hid, 0, hw), (NBLK + j, og, hw, dw)):
+            total = None
+            for h in range(2):
+                term = lax.dot_general(
+                    fac[j, :, pl.ds(h * half + base, width)],
+                    ref[rows, pl.ds(h * width, width)],
+                    (((1,), (1,)), ((), ())),
+                    preferred_element_type=jnp.float32,
+                )
+                total = term if total is None else total + term
+            part[i] = total
+
+    parts[t] = part[t]
+    for o in range(1, NT):
+        peer = lax.rem(t + o, NT)
+        far(part.at[peer], parts.at[t], psum_sem.at[0], psum_sem.at[1], {"tensor": peer}).start()
+    wait_bytes(parts.at[pl.ds(0, NT - 1)], psum_sem.at[1])
+    total = parts[0]
+    for i in range(1, NT):
+        total = total + parts[i]
+    pb[t] = total.astype(jnp.bfloat16)
+    for o in range(1, NT):
+        peer = lax.rem(t + o, NT)
+        far(pb.at[t], pb.at[t], psum_sem.at[2], psum_sem.at[3], {"tensor": peer}).start()
+    wait_bytes(pb.at[pl.ds(0, NT - 1)], psum_sem.at[3])
+
+    for j in range(NBLK):
+        rows = pl.ds(j * BLOCK, BLOCK)
+        for i, ref, base, width in ((NBLK + j, hid, 0, hw), (j, og, hw, dw)):
+            for h in range(2):
+                grad = adapter_scale * jnp.dot(
+                    pb[i], ref[rows, pl.ds(h * width, width)], preferred_element_type=jnp.float32
+                )
+                grads[j, :, pl.ds(h * half + base, width)] = grad.astype(jnp.bfloat16)
+    swap = far(grads.at[:, :, pl.ds(so, half)], items.at[mine8], sib.at[4], sib.at[5], sibling)
+    swap.start()
+    keep = pltpu.make_async_copy(
+        grads, fin.at[pl.ds(pl.multiple_of(2 * SLOTS + core * NBLK, NBLK), NBLK)], loc.at[5]
+    )
+    keep.start()
+    share = far(
+        grads, fin.at[pl.ds(pl.multiple_of(2 * SLOTS + core * NBLK, NBLK), NBLK)], sib.at[6], sib.at[7], sibling
+    )
+    share.start()
+    items[mine8] = grads[:, :, pl.ds(ko, half)]
+    swap.wait_recv()
+    ring(1, items, 2 * NBLK, fin)
+
+    keep.wait()
+    share.wait()
+    swap.wait_send()
+    wait_bytes(idbuf.at[pl.ds(0, NDP - 1)], ids_sem.at[0])
+    wait_bytes(own_r.at[pl.ds(0, OWNED)], sib.at[0])
+    wait_bytes(own_s.at[pl.ds(0, OWNED)], sib.at[2])
+    wait_bytes(parts.at[pl.ds(0, NT - 1)], psum_sem.at[0])
+    wait_bytes(pb.at[pl.ds(0, NT - 1)], psum_sem.at[2])
+    for phase in range(2):
+        wait_bytes(stage.at[phase], ring_send.at[phase])
+        wait_bytes(picked.at[pl.ds(0, 2 * SLOTS), :, pl.ds(0, half)], fwd.at[phase, 1])
+
+
+def last_kernel(hw, dw, table, fin, fac, pb, gh, ga, gb, acc, buf, ghb, gab, gbb, sems):
+    half = hw + dw
+
+    def code_of(p):
+        column = jnp.where(p < SLOTS, 5, jnp.where(p < 2 * SLOTS, 6, 7))
+        row = jnp.where(p < SLOTS, p, jnp.where(p < 2 * SLOTS, p - SLOTS, p - 2 * SLOTS))
+        return table[row, column]
+
+    def fetch(p, carry):
+        @pl.when(code_of(p) > 0)
+        def _():
+            pltpu.make_async_copy(fin.at[p], buf.at[p], sems.at[0]).start()
+
+        return carry
+
+    lax.fori_loop(0, NFIN, fetch, 0)
+    for j in range(NBLK):
+        rows = pl.ds(j * BLOCK, BLOCK)
+        for h in range(2):
+            rows_out = adapter_scale * lax.dot_general(
+                pb[NBLK + j],
+                fac[j, :, pl.ds(h * half, hw)],
+                (((0,), (0,)), ((), ())),
+                preferred_element_type=jnp.float32,
+            )
+            ghb[rows, pl.ds(h * hw, hw)] = rows_out.astype(jnp.bfloat16)
+        pltpu.make_async_copy(ghb.at[rows], gh.at[rows], sems.at[1]).start()
+    acc[...] = jnp.zeros_like(acc)
+
+    def drain(p, carry):
+        @pl.when(code_of(p) > 0)
+        def _():
+            pltpu.make_async_copy(fin.at[p], buf.at[p], sems.at[0]).wait()
+
+        return carry
+
+    lax.fori_loop(0, NFIN, drain, 0)
+
+    def add(p, carry):
+        code = code_of(p)
+
+        @pl.when(code > 0)
+        def _():
+            acc[code - 1] += buf[p].astype(jnp.float32)
+
+        return carry
+
+    lax.fori_loop(0, NFIN, add, 0)
+
+    def write(i, carry):
+        for h in range(2):
+            gab[i, :, pl.ds(h * hw, hw)] = acc[i, :, pl.ds(h * half, hw)].astype(jnp.bfloat16)
+            gbb[i, :, pl.ds(h * dw, dw)] = acc[i, :, pl.ds(h * half + hw, dw)].astype(jnp.bfloat16)
+        return carry
+
+    lax.fori_loop(0, OWNED, write, 0)
+    ca = pltpu.make_async_copy(gab, ga, sems.at[2])
+    cb = pltpu.make_async_copy(gbb, gb, sems.at[3])
+    ca.start()
+    cb.start()
+    pltpu.make_async_copy(ghb, gh, sems.at[1]).wait()
+    ca.wait()
+    cb.wait()
+
+
+def shards(hidden, output_gradient, block_adapter_index, adapter_down_factors, adapter_up_factors):
+    rows, ff_local = hidden.shape
+    d_local = output_gradient.shape[1]
+    hw, dw = ff_local // 2, d_local // 2
+    half = hw + dw
+    wide_ids = jnp.broadcast_to(jnp.tile(block_adapter_index, 16)[None, :], (8, 128))
+    bf16, f32 = jnp.bfloat16, jnp.float32
+    vmem = pl.BlockSpec(memory_space=pltpu.VMEM)
+    anywhere = pl.BlockSpec(memory_space=pl.ANY)
+    dma = pltpu.SemaphoreType.DMA
+    chunk_shapes = [
+        pltpu.VMEM((GROUP, ADAPTER_RANK, width), bf16) for _ in range(4 * CHUNKS) for width in (640, half - 640)
+    ]
+    scratch = [
+        pltpu.VMEM((NDP, 8, 128), jnp.int32),
+        pltpu.SMEM((32, 128), jnp.int32),
+        pltpu.VMEM((2 * OWNED, ADAPTER_RANK, half), bf16),
+        pltpu.VMEM((2 * OWNED, ADAPTER_RANK, half), bf16),
+        pltpu.VMEM((2 * SLOTS, ADAPTER_RANK, 2 * half), bf16),
+        pltpu.VMEM((2, 2, SLOTS, ADAPTER_RANK, half), bf16),
+        pltpu.VMEM((rows, ff_local), bf16),
+        pltpu.VMEM((rows, d_local), bf16),
+        pltpu.VMEM((2 * NBLK, ADAPTER_RANK, BLOCK), f32),
+        pltpu.VMEM((NT, ADAPTER_RANK, BLOCK), f32),
+        pltpu.VMEM((NBLK, ADAPTER_RANK, 2 * half), bf16),
+        pltpu.VMEM((2 * NBLK, ADAPTER_RANK, half), bf16),
+    ]
+    sems = [
+        dma((6,)),
+        dma((2,)),
+        dma((8,)),
+        dma((2,)),
+        dma((2, 2, CHUNKS, 2)),
+        dma((2, 3)),
+        dma((4,)),
+    ]
+    n_scratch, n_chunks = len(scratch), len(chunk_shapes)
+
+    def body(*refs):
+        head = 9 + n_scratch
+        ring_kernel(hw, dw, *refs[:head], refs[head : head + n_chunks], *refs[head + n_chunks :])
+
+    table, fac, pb, fin = pl.pallas_call(
+        body,
+        name="ring",
+        out_shape=(
+            jax.ShapeDtypeStruct((32, 128), jnp.int32),
+            jax.ShapeDtypeStruct((NBLK, ADAPTER_RANK, 2 * half), bf16),
+            jax.ShapeDtypeStruct((2 * NBLK, ADAPTER_RANK, BLOCK), bf16),
+            jax.ShapeDtypeStruct((NFIN, ADAPTER_RANK, 2 * half), bf16),
+        ),
+        in_specs=[vmem, anywhere, anywhere, anywhere, anywhere],
+        out_specs=(vmem, vmem, vmem, anywhere),
+        scratch_shapes=scratch + chunk_shapes + sems,
+        compiler_params=pltpu.CompilerParams(
+            collective_id=0, has_side_effects=True, vmem_limit_bytes=VMEM_LIMIT
+        ),
+    )(wide_ids, hidden, output_gradient, adapter_down_factors, adapter_up_factors)
+
+    def finish(*_):
+        return pl.pallas_call(
+            functools.partial(last_kernel, hw, dw),
+            name="finish",
+            out_shape=(
+                jax.ShapeDtypeStruct((rows, ff_local), bf16),
+                jax.ShapeDtypeStruct(adapter_down_factors.shape, bf16),
+                jax.ShapeDtypeStruct(adapter_up_factors.shape, bf16),
+            ),
+            in_specs=[pl.BlockSpec(memory_space=pltpu.SMEM), anywhere, vmem, vmem],
+            out_specs=(anywhere, anywhere, anywhere),
+            scratch_shapes=[
+                pltpu.VMEM((OWNED, ADAPTER_RANK, 2 * half), f32),
+                pltpu.VMEM((NFIN, ADAPTER_RANK, 2 * half), bf16),
+                pltpu.VMEM((rows, ff_local), bf16),
+                pltpu.VMEM((OWNED, ADAPTER_RANK, ff_local), bf16),
+                pltpu.VMEM((OWNED, ADAPTER_RANK, d_local), bf16),
+                dma((4,)),
+            ],
+            compiler_params=pltpu.CompilerParams(vmem_limit_bytes=VMEM_LIMIT),
+        )(table, fin, fac, pb)
+
+    return lax.cond(
+        table[0, 8] > 0,
+        finish,
+        general,
+        hidden,
+        output_gradient,
+        block_adapter_index,
+        adapter_down_factors,
+        adapter_up_factors,
+    )
+
+
 def solution(mesh):
     placed = (
         P("dp", "tensor"),

time: 254 us -> 108 us (0.43)
  Pallas kernels: 0 us -> 104 us
  waiting for transfers between devices: 87.1 us -> 0 us
  blocking collectives: 76.1 us -> 0 us
  starting transfers between devices: 33.9 us -> 0 us
  local copies, waits for them, and re-layouts: 34.7 us -> 1.94 us
  matrix products: 18.9 us -> 0 us
    pallas_call x0 -> x2, Pallas kernels: none -> 104 us  [the longest x1 96.3 us: shards(): pl.pallas_call(body, name='ring', out_shape=(jax.ShapeDtypeStruct((32, 12...]
    all_to_all x4 -> x0, waiting for transfers between devices: 87.1 us -> none  [the longest x1 39.2 us: shards(): lax.all_to_all(send_a, 'dp', split_axis=0, concat_axis=0, tiled=True)]
    psum x1 -> x0, blocking collectives: 61.4 us -> none  [shards(): proj, back = lax.psum((proj_part, back_part), 'tensor')]
    all_to_all x4 -> x0, starting transfers between devices: 33.9 us -> none  [the longest x1 18.8 us: shards(): lax.all_to_all(back_bb, 'dp', split_axis=0, concat_axis=0, tiled=True)]
    reshape x9 -> x0, local copies, waits for them, and re-layouts: 21.5 us -> none  [the longest x2 9.19 us: shards(): send_a = send_a.reshape(dp_size, CAP, ADAPTER_RANK, ff_local)]
    dot_general x11 -> x0, matrix products: 18.9 us -> none  [the longest x1 3.13 us: shards(): jnp.einsum('jtf,jrf->jtr', hid_blocks, down_factor, preferred_element_typ...]
    unnamed x1 -> x0, blocking collectives: 14.7 us -> none
    unnamed x9 -> x8, local copies, waits for them, and re-layouts: 5.59 us -> 0.01 us
  transfers between devices with their start and end apart: 4 -> 0, of which waited for: 4 -> 0; matrix products, arithmetic and copies ran while one was open for 13% -> 0% of each run, Pallas kernels for 0% -> 0%
where the time goes in v1:
time: 108 us
  Pallas kernels  104 us (96%)
  local copies, waits for them, and re-layouts  1.94 us (2%)
  between operations  1.51 us (1%)
    pallas_call x1, Pallas kernels, shards(): pl.pallas_call(body, name='ring', out_shape=(jax.ShapeDtypeStruct((32, 12...  96.3 us
    pallas_call x1, Pallas kernels, finish(): pl.pallas_call(functools.partial(last_kernel, hw, dw), name='finish', out...  7.64 us

profile of v1, /device:TPU:1, one launch (start us, length us, event | category | flops | bytes accessed | tf_op | source)
XLA Modules:
  0.0 107.7 jit_solution(13569595113362120417)
XLA Ops:
  0.6 0.7 tile.2
  1.3 0.1 broadcast_in_dim.32
  1.4 0.6 broadcast_in_dim.50.refs_0_
  2.0 0.0 copy-start
  2.0 0.0 copy-start.1
  2.0 0.0 copy-start.2
  2.0 0.0 copy-start.3
  2.0 96.3 %ring.1 = (s32[32,128]{1,0:T(8,128)S(1)}, bf16[8,16,2304]{2,1,0:T(8,128)(2,1)}, bf16[16,16,128]{2,1,0:T(8,128)(2,1)S(1)}, bf16[72,16,2304]{2,1,0:T(8,128)(2,1)}) custom-call(s32[8,128]{1,0:T(8,128)} %broadcast_in_dim.50.refs_0_, bf16[1024,1792]{1,0:T(8,128)(2,1)} %refs_1_.1, bf16[1024,512]{1,0:T(8,128)(2,1)} %refs_2_.1, bf16[32,16,1792]{2,1,0:T(8,128)(2,1)} %refs_3_.1, ...), custom_call_target="tpu_custom_call" | custom-call | tf_op jit(solution)/shard_map/ring/pallas_call | solution.py:521
  98.3 0.6 slice.3
  99.6 0.0 copy-done
  99.6 0.0 copy-done.1
  99.6 0.0 copy-done.2
  99.6 0.0 copy-done.3
  99.6 7.9 %conditional.1 = ((bf16[1024,1792]{1,0:T(8,128)(2,1)}, bf16[32,16,1792]{2,1,0:T(8,128)(2,1)}, bf16[32,16,512]{2,1,0:T(8,128)(2,1)})) conditional(s32[]{:T(128)} %bitcast.19, (s32[8]{0:T(128)S(1)}, bf16[32,16,512]{2,1,0:T(8,128)(2,1)S(1)}, bf16[1024,512]{1,0:T(8,128)(2,1)S(1)}, bf16[32,16,1792]{2,1,0:T(8,128)(2,1)S(1)}, ...), branch_computations={%region_0.6_spmd, %region_5.7_spmd} | conditional | flops 387978816 | bytes 71245976 | solution.py:560
  99.8 7.6 %finish.1 = (bf16[1024,1792]{1,0:T(8,128)(2,1)}, bf16[32,16,1792]{2,1,0:T(8,128)(2,1)}, bf16[32,16,512]{2,1,0:T(8,128)(2,1)}) custom-call(s32[32,128]{1,0:T(8,128)S(1)} %get-tuple-element.24.table, bf16[72,16,2304]{2,1,0:T(8,128)(2,1)} %get-tuple-element.25.fin, bf16[8,16,2304]{2,1,0:T(8,128)(2,1)} %get-tuple-element.26.fac, ...), custom_call_target="tpu_custom_call" | custom-call | tf_op jit(solution)/shard_map/cond/branch_1_fun/finish/pallas_call | solution.py:539
Async XLA Ops:
  2.0 97.6 %copy-start = (bf16[1024,512]{1,0:T(8,128)(2,1)S(1)}, bf16[1024,512]{1,0:T(8,128)(2,1)}, u32[]{:S(2)}) copy-start(bf16[1024,512]{1,0:T(8,128)(2,1)} %refs_2_.1) | copy-start | bytes 3145732
  2.0 97.6 %copy-start.1 = (bf16[32,16,1792]{2,1,0:T(8,128)(2,1)S(1)}, bf16[32,16,1792]{2,1,0:T(8,128)(2,1)}, u32[]{:S(2)}) copy-start(bf16[32,16,1792]{2,1,0:T(8,128)(2,1)} %refs_3_.1) | copy-start | bytes 5505028
  2.0 97.6 %copy-start.2 = (bf16[32,16,512]{2,1,0:T(8,128)(2,1)S(1)}, bf16[32,16,512]{2,1,0:T(8,128)(2,1)}, u32[]{:S(2)}) copy-start(bf16[32,16,512]{2,1,0:T(8,128)(2,1)} %refs_4_.1) | copy-start | bytes 1572868
  2.0 97.6 %copy-start.3 = (s32[8]{0:T(128)S(1)}, s32[8]{0:T(128)}, u32[]{:S(2)}) copy-start(s32[8]{0:T(128)} %param.11) | copy-start | bytes 100

commit v2 on v1

--- a/solution.py
+++ b/solution.py
@@ -17,7 +17,9 @@
 NBLK = 8
 OWNED = 32
 SLOTS = 28
-GROUP = 4
+GROUP = 2
+BEHIND = 3
+LAG = GROUP * BEHIND
 CHUNKS = SLOTS // GROUP
 NFIN = 2 * SLOTS + 16
 VMEM_LIMIT = 56 * 1024 * 1024
@@ -167,7 +169,7 @@
             starts.append(
                 jnp.maximum(
                     starts[h - 1] + shifted(counts[h - 1], h - 1),
-                    shifted(starts[h - 1], 1) + GROUP,
+                    shifted(starts[h - 1], 1) + LAG,
                 )
             )
         for h in range(4):
@@ -204,7 +206,6 @@
     owner_chip = ids >> 6
     chip_slot = ids & 63
     mine = (ids >> 5) == me
-    row = (ids & 31) + 1
     fetch, longest_f = slot_plan(owner_chip, token_chip, chip_slot, chip, sub, lane)
     back, longest_b = slot_plan(token_chip, owner_chip, lane & 15, chip, sub, lane)
     fits = jnp.max(jnp.maximum(longest_f, longest_b), axis=0, keepdims=True) <= SLOTS
@@ -216,15 +217,23 @@
     for d in range(2):
         where = jnp.where(fetch[d][3], 65 + d * SLOTS + fetch[d][4], where)
     columns.append(by_row((lane >> 3) == me, lane & 7, where, 32))
+    stays = jnp.logical_and(owner_chip == token_chip, token_chip == chip)
+    landing = jnp.where(stays, 2 * SLOTS + (lane & 15), -1)
     for d in range(2):
-        columns.append(by_row(jnp.logical_and(back[d][3], mine), back[d][4], row, 32))
-    stays = jnp.logical_and(jnp.logical_and(owner_chip == token_chip, token_chip == chip), mine)
-    columns.append(by_row(stays, lane & 15, row, 32))
+        landing = jnp.where(back[d][3], d * SLOTS + back[d][4], landing)
+    wanted = jnp.logical_and(landing >= 0, mine)
+    count = bcast(jnp.sum(jnp.where(wanted, 1, 0), axis=1, keepdims=True))
+    line = lax.broadcasted_iota(jnp.int32, (128, 128), 1)
+    ahead = jnp.transpose(jnp.concatenate([jnp.where(wanted, lane, 128)] * 16, axis=0))
+    rank = bcast(jnp.sum(jnp.where(ahead < line, 1, 0), axis=0, keepdims=True))
+    entry = jnp.where(wanted, rank * 4096 + landing * 32 + (ids & 31), -1)
+    entry = jnp.transpose(jnp.concatenate([entry] * 16, axis=0))
+    listed = bcast(jnp.sum(jnp.where((entry >> 12) == line, entry & 4095, 0), axis=0, keepdims=True))
     wide_lane = lax.broadcasted_iota(jnp.int32, (32, 128), 1)
     table = jnp.where(jnp.broadcast_to(fits, (32, 128)), 1, 0)
     for i, column in enumerate(columns):
         table = jnp.where(wide_lane == i, jnp.broadcast_to(column, (32, 128)), table)
-    return table
+    return jnp.concatenate([table, jnp.where(sub == 0, listed, count)], axis=0)
 
 
 def wait_bytes(ref, sem):
@@ -232,10 +241,9 @@
 
 
 def ring_kernel(hw, dw, ids_ref, hid_hbm, og_hbm, a_hbm, b_hbm, table_ref, fac, pb, fin,
-                idbuf, table, own_r, own_s, picked, stage, hid, og, part, parts, grads, items, arrivals,
+                idbuf, table, own_r, own_s, picked, stage, hid, og, part, parts, grads, items, arrived, kept,
                 loc, ids_sem, sib, ring_send, ring_recv, fwd, psum_sem):
     half = hw + dw
-    pieces = ((0, 640), (640, half - 640))
     me = lax.axis_index("dp")
     t = lax.axis_index("tensor")
     chip = me // 2
@@ -255,6 +263,11 @@
     def cut(ref, width, which):
         return ref.at[:, :, pl.ds(pl.multiple_of(which * width, 128), width)]
 
+    barrier = pltpu.get_barrier_semaphore()
+    for o in range(1, NDP):
+        pl.semaphore_signal(barrier, inc=1, device_id={"dp": lax.rem(me + o, NDP)}, device_id_type=MESH)
+    for o in range(1, NT):
+        pl.semaphore_signal(barrier, inc=1, device_id={"tensor": lax.rem(t + o, NT)}, device_id_type=MESH)
     for ref, dst, width, at in ((a_hbm, own_r, hw, 0), (b_hbm, own_r, dw, hw)):
         pltpu.make_async_copy(cut(ref, width, core), dst.at[mine32, :, pl.ds(at, width)], loc.at[0]).start()
     for ref, dst, width, at in ((a_hbm, own_s, hw, 0), (b_hbm, own_s, dw, hw)):
@@ -262,13 +275,11 @@
     pltpu.make_async_copy(hid_hbm, hid, loc.at[2]).start()
     pltpu.make_async_copy(og_hbm, og, loc.at[3]).start()
 
-    barrier = pltpu.get_barrier_semaphore()
-    for o in range(1, NDP):
-        pl.semaphore_signal(barrier, inc=1, device_id={"dp": lax.rem(me + o, NDP)}, device_id_type=MESH)
-    for o in range(1, NT):
-        pl.semaphore_signal(barrier, inc=1, device_id={"tensor": lax.rem(t + o, NT)}, device_id_type=MESH)
     lane = lax.broadcasted_iota(jnp.int32, (8, 128), 1)
-    idbuf[me] = jnp.where((lane >> 3) == me, ids_ref[...], 0)
+    mine_ids = jnp.zeros((8, 128), jnp.int32)
+    for j in range(NBLK):
+        mine_ids = jnp.where(lane == me * NBLK + j, ids_ref[j], mine_ids)
+    idbuf[me] = mine_ids
     pl.semaphore_wait(barrier, NDP - 1 + NT - 1)
 
     for o in range(1, NDP):
@@ -288,48 +299,41 @@
     to_smem.wait()
 
     def ring(phase, own, count, land):
-        def chunk(d, q, p):
-            return arrivals[((phase * 2 + d) * CHUNKS + q) * 2 + p]
-
-        def copy(d, q, p):
-            at, width = pieces[p]
+        def copy(d, q):
+            slots = pl.ds(q * GROUP, GROUP)
             return far(
-                stage.at[phase, d, pl.ds(q * GROUP, GROUP), :, pl.ds(at, width)],
-                chunk(d, q, p),
+                stage.at[phase, d, slots],
+                arrived.at[phase, d, slots],
                 ring_send.at[phase],
-                ring_recv.at[phase, d, q, p],
+                ring_recv.at[phase, d, q],
                 {"dp": lax.rem(chip + (1 if d == 0 else NCHIP - 1), NCHIP) * 2 + core},
             )
 
-        def landed(d, q, p):
-            at, width = pieces[p]
-            copy(d, q, p).wait_recv()
-            there = land.at[
-                pl.ds(d * SLOTS + q * GROUP, GROUP), :, pl.ds(pl.multiple_of(ko + at, 128), width)
-            ]
-            pltpu.make_async_copy(chunk(d, q, p), there, fwd.at[phase, 0]).start()
-            far(chunk(d, q, p), there, fwd.at[phase, 1], fwd.at[phase, 2], sibling).start()
-
-        for m in range(CHUNKS):
-            for p in range(2):
-                at, width = pieces[p]
-                for d in range(2):
-                    if m > 0:
-                        landed(d, m - 1, p)
+        def landed(d, q):
+            copy(d, q).wait_recv()
+            slots = pl.ds(q * GROUP, GROUP)
+            there = land.at[pl.ds(d * SLOTS + q * GROUP, GROUP), :, pl.ds(ko, half)]
+            far(arrived.at[phase, d, slots], there, fwd.at[phase, 1], fwd.at[phase, 2], sibling).start()
+            if phase == 1:
+                pltpu.make_async_copy(arrived.at[phase, d, slots], there, fwd.at[phase, 0]).start()
+            kept[pl.ds(d * SLOTS + q * GROUP, GROUP)] = arrived[phase, d, slots]
+
+        for m in range(CHUNKS + BEHIND):
+            for d in range(2):
+                if m >= BEHIND:
+                    landed(d, m - BEHIND)
+                if m < CHUNKS:
                     for i in range(GROUP):
                         code = table[m * GROUP + i, phase * 2 + d]
-                        value = own[jnp.clip(code - 1, 0, count - 1), :, pl.ds(at, width)]
-                        for q in range(m):
-                            place = code - 65 - q * GROUP
-                            inside = jnp.logical_and(place >= 0, place < GROUP)
-                            value = jnp.where(inside, chunk(d, q, p)[jnp.clip(place, 0, GROUP - 1)], value)
-                        stage[phase, d, m * GROUP + i, :, pl.ds(at, width)] = value
-                    copy(d, m, p).start()
-        for p in range(2):
-            for d in range(2):
-                landed(d, CHUNKS - 1, p)
+                        value = own[jnp.clip(code - 1, 0, count - 1)]
+                        if m >= BEHIND:
+                            passed = kept[d * SLOTS + jnp.clip(code - 65, 0, SLOTS - 1)]
+                            value = jnp.where(code > 64, passed, value)
+                        stage[phase, d, m * GROUP + i] = value
+                    copy(d, m).start()
         everything = land.at[pl.ds(0, 2 * SLOTS), :, pl.ds(0, half)]
-        wait_bytes(everything, fwd.at[phase, 0])
+        if phase == 1:
+            wait_bytes(everything, fwd.at[phase, 0])
         wait_bytes(everything, fwd.at[phase, 2])
 
     wait_bytes(own_r.at[pl.ds(0, OWNED)], loc.at[0])
@@ -343,8 +347,8 @@
         near = code <= 64
         at = jnp.clip(code - 1, 0, 2 * OWNED - 1)
         away = jnp.clip(code - 65, 0, 2 * SLOTS - 1)
-        for own, o in ((own_r, ko), (own_s, so)):
-            fac[j, :, pl.ds(o, half)] = jnp.where(near, own[at], picked[away, :, pl.ds(o, half)])
+        fac[j, :, pl.ds(ko, half)] = jnp.where(near, own_r[at], kept[away])
+        fac[j, :, pl.ds(so, half)] = jnp.where(near, own_s[at], picked[away, :, pl.ds(so, half)])
 
     wait_bytes(hid, loc.at[2])
     wait_bytes(og, loc.at[3])
@@ -413,20 +417,19 @@
 
 def last_kernel(hw, dw, table, fin, fac, pb, gh, ga, gb, acc, buf, ghb, gab, gbb, sems):
     half = hw + dw
-
-    def code_of(p):
-        column = jnp.where(p < SLOTS, 5, jnp.where(p < 2 * SLOTS, 6, 7))
-        row = jnp.where(p < SLOTS, p, jnp.where(p < 2 * SLOTS, p - SLOTS, p - 2 * SLOTS))
-        return table[row, column]
-
-    def fetch(p, carry):
-        @pl.when(code_of(p) > 0)
-        def _():
-            pltpu.make_async_copy(fin.at[p], buf.at[p], sems.at[0]).start()
-
-        return carry
-
-    lax.fori_loop(0, NFIN, fetch, 0)
+    count = table[33, 0]
+
+    def arriving(p):
+        return pltpu.make_async_copy(fin.at[table[32, p] >> 5], buf.at[p], sems.at[0])
+
+    def loop(step):
+        def run(p, carry):
+            step(p)
+            return carry
+
+        lax.fori_loop(0, count, run, 0)
+
+    loop(lambda p: arriving(p).start())
     for j in range(NBLK):
         rows = pl.ds(j * BLOCK, BLOCK)
         for h in range(2):
@@ -438,35 +441,26 @@
             )
             ghb[rows, pl.ds(h * hw, hw)] = rows_out.astype(jnp.bfloat16)
         pltpu.make_async_copy(ghb.at[rows], gh.at[rows], sems.at[1]).start()
-    acc[...] = jnp.zeros_like(acc)
-
-    def drain(p, carry):
-        @pl.when(code_of(p) > 0)
-        def _():
-            pltpu.make_async_copy(fin.at[p], buf.at[p], sems.at[0]).wait()
-
-        return carry
-
-    lax.fori_loop(0, NFIN, drain, 0)
-
-    def add(p, carry):
-        code = code_of(p)
-
-        @pl.when(code > 0)
-        def _():
-            acc[code - 1] += buf[p].astype(jnp.float32)
-
-        return carry
-
-    lax.fori_loop(0, NFIN, add, 0)
-
-    def write(i, carry):
+    gab[...] = jnp.zeros_like(gab)
+    gbb[...] = jnp.zeros_like(gbb)
+    empty = jnp.zeros(acc.shape[1:], jnp.float32)
+
+    def clear(p):
+        acc[table[32, p] & 31] = empty
+
+    def add(p):
+        acc[table[32, p] & 31] += buf[p].astype(jnp.float32)
+
+    def store(p):
+        i = table[32, p] & 31
         for h in range(2):
             gab[i, :, pl.ds(h * hw, hw)] = acc[i, :, pl.ds(h * half, hw)].astype(jnp.bfloat16)
             gbb[i, :, pl.ds(h * dw, dw)] = acc[i, :, pl.ds(h * half + hw, dw)].astype(jnp.bfloat16)
-        return carry
-
-    lax.fori_loop(0, OWNED, write, 0)
+
+    loop(clear)
+    loop(lambda p: arriving(p).wait())
+    loop(add)
+    loop(store)
     ca = pltpu.make_async_copy(gab, ga, sems.at[2])
     cb = pltpu.make_async_copy(gbb, gb, sems.at[3])
     ca.start()
@@ -481,17 +475,13 @@
     d_local = output_gradient.shape[1]
     hw, dw = ff_local // 2, d_local // 2
     half = hw + dw
-    wide_ids = jnp.broadcast_to(jnp.tile(block_adapter_index, 16)[None, :], (8, 128))
     bf16, f32 = jnp.bfloat16, jnp.float32
     vmem = pl.BlockSpec(memory_space=pltpu.VMEM)
     anywhere = pl.BlockSpec(memory_space=pl.ANY)
     dma = pltpu.SemaphoreType.DMA
-    chunk_shapes = [
-        pltpu.VMEM((GROUP, ADAPTER_RANK, width), bf16) for _ in range(4 * CHUNKS) for width in (640, half - 640)
-    ]
     scratch = [
         pltpu.VMEM((NDP, 8, 128), jnp.int32),
-        pltpu.SMEM((32, 128), jnp.int32),
+        pltpu.SMEM((40, 128), jnp.int32),
         pltpu.VMEM((2 * OWNED, ADAPTER_RANK, half), bf16),
         pltpu.VMEM((2 * OWNED, ADAPTER_RANK, half), bf16),
         pltpu.VMEM((2 * SLOTS, ADAPTER_RANK, 2 * half), bf16),
@@ -502,38 +492,34 @@
         pltpu.VMEM((NT, ADAPTER_RANK, BLOCK), f32),
         pltpu.VMEM((NBLK, ADAPTER_RANK, 2 * half), bf16),
         pltpu.VMEM((2 * NBLK, ADAPTER_RANK, half), bf16),
+        pltpu.VMEM((2, 2, SLOTS, ADAPTER_RANK, half), bf16),
+        pltpu.VMEM((2 * SLOTS, ADAPTER_RANK, half), bf16),
     ]
     sems = [
         dma((6,)),
         dma((2,)),
         dma((8,)),
         dma((2,)),
-        dma((2, 2, CHUNKS, 2)),
+        dma((2, 2, CHUNKS)),
         dma((2, 3)),
         dma((4,)),
     ]
-    n_scratch, n_chunks = len(scratch), len(chunk_shapes)
-
-    def body(*refs):
-        head = 9 + n_scratch
-        ring_kernel(hw, dw, *refs[:head], refs[head : head + n_chunks], *refs[head + n_chunks :])
-
     table, fac, pb, fin = pl.pallas_call(
-        body,
+        functools.partial(ring_kernel, hw, dw),
         name="ring",
         out_shape=(
-            jax.ShapeDtypeStruct((32, 128), jnp.int32),
+            jax.ShapeDtypeStruct((40, 128), jnp.int32),
             jax.ShapeDtypeStruct((NBLK, ADAPTER_RANK, 2 * half), bf16),
             jax.ShapeDtypeStruct((2 * NBLK, ADAPTER_RANK, BLOCK), bf16),
             jax.ShapeDtypeStruct((NFIN, ADAPTER_RANK, 2 * half), bf16),
         ),
-        in_specs=[vmem, anywhere, anywhere, anywhere, anywhere],
+        in_specs=[pl.BlockSpec(memory_space=pltpu.SMEM)] + [anywhere] * 4,
         out_specs=(vmem, vmem, vmem, anywhere),
-        scratch_shapes=scratch + chunk_shapes + sems,
+        scratch_shapes=scratch + sems,
         compiler_params=pltpu.CompilerParams(
             collective_id=0, has_side_effects=True, vmem_limit_bytes=VMEM_LIMIT
         ),
-    )(wide_ids, hidden, output_gradient, adapter_down_factors, adapter_up_factors)
+    )(block_adapter_index, hidden, output_gradient, adapter_down_factors, adapter_up_factors)
 
     def finish(*_):
         return pl.pallas_call(

time: 108 us -> 91.3 us (0.85)
  Pallas kernels: 104 us -> 88.8 us
  local copies, waits for them, and re-layouts: 1.94 us -> 0.6 us
    pallas_call x1, Pallas kernels: 96.3 us -> 84.7 us  [shards(): pl.pallas_call(functools.partial(ring_kernel, hw, dw), name='ring', out_s...]
    pallas_call x1, Pallas kernels: 7.64 us -> 4.08 us  [finish(): pl.pallas_call(functools.partial(last_kernel, hw, dw), name='finish', out...]
where the time goes in v2:
time: 91.3 us; the launch traced here: 91.1 us
  Pallas kernels  88.8 us (97%)
  between operations  1.54 us (2%)
    pallas_call x1, Pallas kernels, shards(): pl.pallas_call(functools.partial(ring_kernel, hw, dw), name='ring', out_s...  84.7 us
    pallas_call x1, Pallas kernels, finish(): pl.pallas_call(functools.partial(last_kernel, hw, dw), name='finish', out...  4.08 us

profile of v2, /device:TPU:1, one launch (start us, length us, event | category | flops | bytes accessed | tf_op | source)
XLA Modules:
  0.0 91.1 jit_solution(9745631544674674567)
XLA Ops:
  0.6 0.0 copy-start
  0.6 0.0 copy-start.1
  0.7 0.0 copy-start.2
  0.7 0.0 copy-start.3
  0.7 84.7 %ring.1 = (s32[40,128]{1,0:T(8,128)S(1)}, bf16[8,16,2304]{2,1,0:T(8,128)(2,1)}, bf16[16,16,128]{2,1,0:T(8,128)(2,1)S(1)}, bf16[72,16,2304]{2,1,0:T(8,128)(2,1)}) custom-call(s32[8]{0:T(128)} %ids_ref.1, bf16[1024,1792]{1,0:T(8,128)(2,1)} %hid_hbm.1, bf16[1024,512]{1,0:T(8,128)(2,1)} %og_hbm.1, bf16[32,16,1792]{2,1,0:T(8,128)(2,1)} %a_hbm.1, ...), custom_call_target="tpu_custom_call" | custom-call | tf_op jit(solution)/shard_map/ring/pallas_call | solution.py:507
  85.4 0.6 slice.3
  86.6 0.0 copy-done
  86.6 0.0 copy-done.1
  86.6 0.0 copy-done.2
  86.6 0.0 copy-done.3
  86.6 4.3 %conditional.1 = ((bf16[1024,1792]{1,0:T(8,128)(2,1)}, bf16[32,16,1792]{2,1,0:T(8,128)(2,1)}, bf16[32,16,512]{2,1,0:T(8,128)(2,1)})) conditional(s32[]{:T(128)} %bitcast.19, (s32[8]{0:T(128)S(1)}, bf16[32,16,512]{2,1,0:T(8,128)(2,1)S(1)}, bf16[1024,512]{1,0:T(8,128)(2,1)S(1)}, bf16[32,16,1792]{2,1,0:T(8,128)(2,1)S(1)}, ...), branch_computations={%region_0.6_spmd, %region_5.7_spmd} | conditional | flops 387978816 | bytes 71245976 | solution.py:546
  86.9 4.1 %finish.1 = (bf16[1024,1792]{1,0:T(8,128)(2,1)}, bf16[32,16,1792]{2,1,0:T(8,128)(2,1)}, bf16[32,16,512]{2,1,0:T(8,128)(2,1)}) custom-call(s32[40,128]{1,0:T(8,128)S(1)} %get-tuple-element.24.table, bf16[72,16,2304]{2,1,0:T(8,128)(2,1)} %get-tuple-element.25.fin, bf16[8,16,2304]{2,1,0:T(8,128)(2,1)} %get-tuple-element.26.fac, ...), custom_call_target="tpu_custom_call" | custom-call | tf_op jit(solution)/shard_map/cond/branch_1_fun/finish/pallas_call | solution.py:525
Async XLA Ops:
  0.6 86.0 %copy-start = (bf16[1024,512]{1,0:T(8,128)(2,1)S(1)}, bf16[1024,512]{1,0:T(8,128)(2,1)}, u32[]{:S(2)}) copy-start(bf16[1024,512]{1,0:T(8,128)(2,1)} %og_hbm.1) | copy-start | bytes 3145732
  0.6 86.0 %copy-start.1 = (bf16[32,16,1792]{2,1,0:T(8,128)(2,1)S(1)}, bf16[32,16,1792]{2,1,0:T(8,128)(2,1)}, u32[]{:S(2)}) copy-start(bf16[32,16,1792]{2,1,0:T(8,128)(2,1)} %a_hbm.1) | copy-start | bytes 5505028
  0.7 86.0 %copy-start.2 = (bf16[32,16,512]{2,1,0:T(8,128)(2,1)S(1)}, bf16[32,16,512]{2,1,0:T(8,128)(2,1)}, u32[]{:S(2)}) copy-start(bf16[32,16,512]{2,1,0:T(8,128)(2,1)} %b_hbm.1) | copy-start | bytes 1572868
  0.7 86.0 %copy-start.3 = (s32[8]{0:T(128)S(1)}, s32[8]{0:T(128)}, u32[]{:S(2)}) copy-start(s32[8]{0:T(128)} %ids_ref.1) | copy-start | bytes 100

commit v3 on v0

--- a/solution.py
+++ b/solution.py
@@ -1,17 +1,34 @@
+import functools
+
 import jax
 import jax.numpy as jnp
 from jax import lax
+from jax.experimental import pallas as pl
+from jax.experimental.pallas import tpu as pltpu
 from jax.sharding import PartitionSpec as P
 
 ADAPTER_RANK = 16
 BLOCK = 128
 CAP = 2
+MESH = pl.DeviceIdType.MESH
+NDP = 16
+NCHIP = 8
+NT = 16
+NBLK = 8
+OWNED = 32
+SLOTS_OUT = 25
+SLOTS_BACK = 26
+LAG = 6
+NFIN = 2 * SLOTS_BACK + 16
+ORDER_OUT = "bbbabbbababbababbababababaPaaaaRaa"
+ORDER_BACK = "aaSaaaaGXbabbababbababbababbababbab"
+VMEM_LIMIT = 56 * 1024 * 1024
 
 
 adapter_scale = 2.0
 
 
-def shards(hidden, output_gradient, block_adapter_index, adapter_down_factors, adapter_up_factors):
+def general(hidden, output_gradient, block_adapter_index, adapter_down_factors, adapter_up_factors):
     dp_size = lax.axis_size("dp")
     my_index = lax.axis_index("dp")
     block_count = block_adapter_index.shape[0]
@@ -110,6 +127,560 @@
     return (grad_hidden, grad_a.astype(jnp.bfloat16), grad_b.astype(jnp.bfloat16))
 
 
+def bcast(x, shape=(8, 128)):
+    return jnp.broadcast_to(x, shape)
+
+
+def pick_row(x, sub, row):
+    return bcast(jnp.sum(jnp.where(sub == row, x, 0), axis=0, keepdims=True))
+
+
+def turn(x, by):
+    by = by % 8
+    return pltpu.roll(x, by, 0) if by else x
+
+
+def tall(x):
+    return jnp.concatenate([x] * 16, axis=0)
+
+
+def slot_plan(src, dst, own_index, shared, chip, sub, lane):
+    ahead = (dst - src) & 7
+    low = lax.broadcasted_iota(jnp.int32, (128, 128), 0)
+    line = lax.broadcasted_iota(jnp.int32, (128, 128), 1)
+
+    def per_chip(mask):
+        return bcast(jnp.sum(jnp.where(jnp.logical_and(src == sub, mask), 1, 0), axis=1, keepdims=True))
+
+    def over_all(x):
+        return bcast(jnp.sum(x, axis=0, keepdims=True))
+
+    one, two, three, across, five, six, seven = [per_chip(ahead == d) for d in range(1, 8)]
+    load_p = one + two + three + turn(two + three, 1) + turn(three, 2)
+    load_m = seven + six + five + turn(six + five, -1) + turn(five, -2)
+    forward = jnp.zeros((8, 128), jnp.int32)
+    for phase in range(4):
+        worst_p = jnp.maximum(load_p, turn(load_p, -1))
+        worst_p = jnp.maximum(worst_p, turn(worst_p, -2))
+        worst_m = jnp.maximum(load_m, turn(load_m, 1))
+        worst_m = jnp.maximum(worst_m, turn(worst_m, 2))
+        share = jnp.minimum(jnp.maximum((across + worst_m - worst_p + 1) >> 1, 0), across)
+        chosen = (sub & 3) == phase
+        share_p = jnp.where(chosen, share, 0)
+        share_m = jnp.where(chosen, across - share, 0)
+        forward = forward + share_p
+        share_p = share_p + turn(share_p, 1)
+        load_p = load_p + share_p + turn(share_p, 2)
+        share_m = share_m + turn(share_m, -1)
+        load_m = load_m + share_m + turn(share_m, -2)
+    opposite = tall(jnp.where(ahead == 4, src, 8))
+    nth = over_all(jnp.where(jnp.logical_and(jnp.transpose(opposite) == opposite, low < line), 1, 0))
+    quota = over_all(jnp.where(src == sub, forward, 0))
+    plus = jnp.logical_and(ahead > 0, jnp.logical_or(ahead < 4, jnp.logical_and(ahead == 4, nth < quota)))
+    minus = jnp.logical_or(ahead > 4, jnp.logical_and(ahead == 4, nth >= quota))
+    dist = jnp.where(plus, ahead, jnp.where(minus, 8 - ahead, 0))
+    group = jnp.where(ahead > 0, src * 2 + jnp.where(minus, 1, 0), 16)
+    order = group * 1024 + (4 - dist) * 128 + lane
+    wide = tall(order)
+    if shared is None:
+        active = lane >= 0
+    else:
+        packed = tall(shared * 32768 + order)
+        column = jnp.transpose(packed)
+        same = (packed >> 10) == (column >> 10)
+        active = over_all(jnp.where(jnp.logical_and(same, column < packed), 1, 0)) == 0
+    column = jnp.transpose(tall(jnp.where(active, order, 32767)))
+    rank = over_all(jnp.where(jnp.logical_and((column >> 10) == (wide >> 10), column < wide), 1, 0))
+    if shared is not None:
+        led = jnp.transpose(tall(jnp.where(active, rank, 0)))
+        rank = over_all(jnp.where(same, led, 0))
+    result = []
+    longest = jnp.zeros((8, 128), jnp.int32)
+    for sign, act in ((1, plus), (-1, minus)):
+        goes = jnp.logical_and(act, active)
+        counts = [per_chip(jnp.logical_and(goes, dist > h)) for h in range(4)]
+        starts = [jnp.zeros((8, 128), jnp.int32)]
+        for h in range(1, 4):
+            starts.append(
+                jnp.maximum(
+                    starts[h - 1] + turn(counts[h - 1], sign * (h - 1)),
+                    turn(starts[h - 1], sign) + LAG,
+                )
+            )
+        for h in range(4):
+            here = turn(counts[h], sign * h)
+            longest = jnp.maximum(longest, jnp.where(here > 0, starts[h] + here, 0))
+        age = (sign * (chip - src)) & 7
+        out_start = jnp.zeros((8, 128), jnp.int32)
+        in_start = jnp.zeros((8, 128), jnp.int32)
+        before_chip = (chip - sign) & 7
+        for h in range(4):
+            out_start = jnp.where(age == h, pick_row(starts[h], sub, chip), out_start)
+            in_start = jnp.where(age == h + 1, pick_row(starts[h], sub, before_chip), in_start)
+        leaves = jnp.logical_and(goes, age < dist)
+        arrives = jnp.logical_and(act, age == dist)
+        out_slot = out_start + rank
+        in_slot = in_start + rank
+        source = jnp.where(age == 0, own_index + 1, 65 + in_slot)
+        result.append((leaves, out_slot, source, arrives, in_slot))
+    return result, bcast(jnp.max(longest, axis=0, keepdims=True))
+
+
+def by_row(mask, place, value, rows):
+    reps = rows // 8
+    wide = [jnp.concatenate([v] * reps, axis=0) for v in (jnp.where(mask, place, -1), value)]
+    sub = lax.broadcasted_iota(jnp.int32, (rows, 128), 0)
+    return jnp.sum(jnp.where(wide[0] == sub, wide[1], 0), axis=1, keepdims=True)
+
+
+def make_tables(ids, me):
+    chip = me // 2
+    sub = lax.broadcasted_iota(jnp.int32, (8, 128), 0)
+    lane = lax.broadcasted_iota(jnp.int32, (8, 128), 1)
+    token_chip = lane >> 4
+    owner_chip = ids >> 6
+    chip_slot = ids & 63
+    mine = (ids >> 5) == me
+    fetch, longest_f = slot_plan(owner_chip, token_chip, chip_slot, ids, chip, sub, lane)
+    back, longest_b = slot_plan(token_chip, owner_chip, lane & 15, None, chip, sub, lane)
+    fits = jnp.logical_and(longest_f <= SLOTS_OUT, longest_b <= SLOTS_BACK)
+    columns = []
+    for plan in (fetch, back):
+        for leaves, out_slot, source, _, _ in plan:
+            columns.append(by_row(leaves, out_slot, source, 32))
+    where = jnp.where(owner_chip == token_chip, chip_slot + 1, 0)
+    for d in range(2):
+        where = jnp.where(fetch[d][3], 65 + d * SLOTS_OUT + fetch[d][4], where)
+    columns.append(by_row((lane >> 3) == me, lane & 7, where, 32))
+    stays = jnp.logical_and(owner_chip == token_chip, token_chip == chip)
+    landing = jnp.where(stays, 2 * SLOTS_BACK + (lane & 15), -1)
+    for d in range(2):
+        landing = jnp.where(back[d][3], d * SLOTS_BACK + back[d][4], landing)
+    wanted = jnp.logical_and(landing >= 0, mine)
+    count = bcast(jnp.sum(jnp.where(wanted, 1, 0), axis=1, keepdims=True))
+    line = lax.broadcasted_iota(jnp.int32, (128, 128), 1)
+    ahead = jnp.transpose(jnp.concatenate([jnp.where(wanted, lane, 128)] * 16, axis=0))
+    rank = bcast(jnp.sum(jnp.where(ahead < line, 1, 0), axis=0, keepdims=True))
+    entry = jnp.where(wanted, rank * 4096 + landing * 32 + (ids & 31), -1)
+    entry = jnp.transpose(jnp.concatenate([entry] * 16, axis=0))
+    listed = bcast(jnp.sum(jnp.where((entry >> 12) == line, entry & 4095, 0), axis=0, keepdims=True))
+    wide_lane = lax.broadcasted_iota(jnp.int32, (32, 128), 1)
+    table = jnp.concatenate([jnp.where(fits, 1, 0)] * 4, axis=0)
+    for i, column in enumerate(columns):
+        table = jnp.where(wide_lane == i, jnp.broadcast_to(column, (32, 128)), table)
+    return jnp.concatenate([table, jnp.where(sub == 0, listed, count)], axis=0)
+
+
+def wait_bytes(ref, sem):
+    pltpu.make_async_copy(ref, ref, sem).wait()
+
+
+def ring_kernel(hw, dw, ids_ref, hid_hbm, og_hbm, a_hbm, b_hbm, table_ref, fac_a, back_ref, fin_a, fin_b,
+                idbuf, table, fac_b, proj_ref, hid, og, grads_a, grads_b,
+                own_ra, own_rb, own_sa, own_sb, picked_a, picked_b, items_a, items_b,
+                stage_fa, stage_fb, stage_ra, stage_rb, got_fa, got_fb, got_ra, got_rb, kept_a, kept_b,
+                part, parts, sums, loc, ids_sem, sib, swap_sem, ring_send, ring_recv, fwd, psum_sem):
+    me = lax.axis_index("dp")
+    t = lax.axis_index("tensor")
+    chip = me // 2
+    core = me % 2
+    other = 1 - core
+    sibling = {"dp": chip * 2 + other}
+    mine32 = pl.ds(pl.multiple_of(core * OWNED, OWNED), OWNED)
+    mine8 = pl.ds(pl.multiple_of(core * NBLK, NBLK), NBLK)
+
+    def far(src, dst, send, recv, where):
+        return pltpu.make_async_remote_copy(
+            src_ref=src, dst_ref=dst, send_sem=send, recv_sem=recv, device_id=where, device_id_type=MESH
+        )
+
+    def lanes(width, which):
+        return pl.ds(pl.multiple_of(which * width, 128), width)
+
+    def cut(ref, width, which):
+        return ref.at[:, :, lanes(width, which)]
+
+    barrier = pltpu.get_barrier_semaphore()
+    for o in range(1, NDP):
+        pl.semaphore_signal(barrier, inc=1, device_id={"dp": lax.rem(me + o, NDP)}, device_id_type=MESH)
+    for o in range(1, NT):
+        pl.semaphore_signal(barrier, inc=1, device_id={"tensor": lax.rem(t + o, NT)}, device_id_type=MESH)
+    owns = ((b_hbm, own_rb, dw, core), (a_hbm, own_ra, hw, core), (b_hbm, own_sb, dw, other), (a_hbm, own_sa, hw, other))
+    for i, (ref, dst, width, which) in enumerate(owns):
+        pltpu.make_async_copy(cut(ref, width, which), dst.at[mine32], loc.at[i]).start()
+    pltpu.make_async_copy(og_hbm, og, loc.at[4]).start()
+    pltpu.make_async_copy(hid_hbm, hid, loc.at[5]).start()
+
+    lane = lax.broadcasted_iota(jnp.int32, (8, 128), 1)
+    mine_ids = jnp.zeros((8, 128), jnp.int32)
+    for j in range(NBLK):
+        mine_ids = jnp.where(lane == me * NBLK + j, ids_ref[j], mine_ids)
+    idbuf[me] = mine_ids
+    pl.semaphore_wait(barrier, NDP - 1 + NT - 1)
+
+    for o in range(1, NDP):
+        far(idbuf.at[me], idbuf.at[me], ids_sem.at[0], ids_sem.at[1], {"dp": lax.rem(me + o, NDP)}).start()
+    for i, (ref, dst, width, which) in enumerate(owns):
+        far(cut(ref, width, 1 - which), dst.at[mine32], sib.at[0, i], sib.at[1, i], sibling).start()
+
+    def own_ready(i):
+        dst = owns[i][1].at[pl.ds(0, OWNED)]
+        wait_bytes(dst, loc.at[i])
+        wait_bytes(dst, sib.at[1, i])
+
+    wait_bytes(idbuf.at[pl.ds(0, NDP - 1)], ids_sem.at[1])
+    ids = idbuf[0]
+    for i in range(1, NDP):
+        ids = ids + idbuf[i]
+    table_ref[...] = make_tables(ids, me)
+    to_smem = pltpu.make_async_copy(table_ref, table, loc.at[6])
+    to_smem.start()
+    to_smem.wait()
+
+    def stream(index, phase, own, stage, got, kept, land_at, keep_local, group):
+        count = own.shape[0]
+        slots = stage.shape[1]
+        behind = LAG // group
+        chunks = [(p, min(group, slots - p)) for p in range(0, slots, group)]
+        everything = kept.at[pl.ds(0, 2 * slots)]
+
+        def copy(d, q):
+            p, n = chunks[q]
+            return far(
+                stage.at[d, pl.ds(p, n)],
+                got.at[d, pl.ds(p, n)],
+                ring_send.at[index],
+                ring_recv.at[index, d, q],
+                {"dp": lax.rem(chip + (1 if d == 0 else NCHIP - 1), NCHIP) * 2 + core},
+            )
+
+        def landed(d, q):
+            copy(d, q).wait_recv()
+            p, n = chunks[q]
+            there = land_at(pl.ds(d * slots + p, n))
+            far(got.at[d, pl.ds(p, n)], there, fwd.at[index, 1], fwd.at[index, 2], sibling).start()
+            if keep_local:
+                pltpu.make_async_copy(got.at[d, pl.ds(p, n)], there, fwd.at[index, 0]).start()
+            kept[pl.ds(d * slots + p, n)] = got[d, pl.ds(p, n)]
+
+        def step(m):
+            for d in range(2):
+                if m >= behind:
+                    landed(d, m - behind)
+                if m < len(chunks):
+                    p, n = chunks[m]
+                    for i in range(n):
+                        code = table[p + i, phase * 2 + d]
+                        value = own[jnp.clip(code - 1, 0, count - 1)]
+                        if m >= behind:
+                            passed = kept[d * slots + jnp.clip(code - 65, 0, slots - 1)]
+                            value = jnp.where(code > 64, passed, value)
+                        stage[d, p + i] = value
+                    copy(d, m).start()
+
+        def arrived():
+            if keep_local:
+                wait_bytes(everything, fwd.at[index, 0])
+            wait_bytes(everything, fwd.at[index, 2])
+
+        def finish():
+            wait_bytes(stage, ring_send.at[index])
+            wait_bytes(everything, fwd.at[index, 1])
+
+        return step, arrived, finish
+
+    def play(order, a, b, **others):
+        step = {"a": 0, "b": 0}
+        for kind in order:
+            if kind in others:
+                others[kind]()
+            else:
+                (a if kind == "a" else b)(step[kind])
+                step[kind] += 1
+
+    fa, fa_arrived, fa_finish = stream(
+        0, 0, own_ra, stage_fa, got_fa, kept_a, lambda s: picked_a.at[s], False, 2
+    )
+    fb, fb_arrived, fb_finish = stream(
+        1, 0, own_rb, stage_fb, got_fb, kept_b, lambda s: picked_b.at[s], False, 2
+    )
+    ra, ra_arrived, ra_finish = stream(
+        2, 1, items_a, stage_ra, got_ra, kept_a, lambda s: fin_a.at[s, :, lanes(hw, core)], True, 2
+    )
+    rb, rb_arrived, rb_finish = stream(
+        3, 1, items_b, stage_rb, got_rb, kept_b, lambda s: fin_b.at[s, :, lanes(dw, core)], True, 2
+    )
+
+    def choose(j, fac, own_r, own_s, kept, picked, width):
+        code = table[j, 4]
+        near = code <= 64
+        at = jnp.clip(code - 1, 0, 2 * OWNED - 1)
+        away = jnp.clip(code - 65, 0, 2 * SLOTS_OUT - 1)
+        fac[j, :, lanes(width, core)] = jnp.where(near, own_r[at], kept[away])
+        fac[j, :, lanes(width, other)] = jnp.where(near, own_s[at], picked[away])
+
+    def project(i, fac, rows_ref):
+        for j in range(NBLK):
+            term = lax.dot_general(
+                fac[j], rows_ref[pl.ds(j * BLOCK, BLOCK)], (((1,), (1,)), ((), ())),
+                preferred_element_type=jnp.float32,
+            )
+            part[i, 2 * j] = term[:8]
+            part[i, 2 * j + 1] = term[8:]
+
+    def peers():
+        return [lax.rem(t + o, NT) for o in range(1, NT)]
+
+    def scatter(i):
+        parts[i, t] = part[i, t]
+        for peer in peers():
+            far(part.at[i, peer], parts.at[i, t], psum_sem.at[i, 0], psum_sem.at[i, 1], {"tensor": peer}).start()
+
+    def reduce(i):
+        wait_bytes(parts.at[i, pl.ds(0, NT - 1)], psum_sem.at[i, 1])
+        total = parts[i, 0]
+        for n in range(1, NT):
+            total = total + parts[i, n]
+        sums[i, t] = total
+        for peer in peers():
+            far(sums.at[i, t], sums.at[i, t], psum_sem.at[i, 2], psum_sem.at[i, 3], {"tensor": peer}).start()
+
+    def gather(i, out):
+        wait_bytes(sums.at[i, pl.ds(0, NT - 1)], psum_sem.at[i, 3])
+        for j in range(NBLK):
+            out[j] = jnp.concatenate([sums[i, 2 * j], sums[i, 2 * j + 1]], axis=0).astype(jnp.bfloat16)
+
+    def gradient(low, rows_ref, grads, width, which):
+        for j in range(NBLK):
+            grad = adapter_scale * jnp.dot(
+                low[j], rows_ref[pl.ds(j * BLOCK, BLOCK), lanes(width, which)], preferred_element_type=jnp.float32
+            )
+            grads[j, :, lanes(width, which)] = grad.astype(jnp.bfloat16)
+
+    tail8 = pl.ds(2 * SLOTS_BACK + core * NBLK, NBLK)
+
+    def hand_over(i, low, rows_ref, grads, items, fin, width):
+        gradient(low, rows_ref, grads, width, other)
+        swap = far(cut(grads, width, other), items.at[mine8], swap_sem.at[i, 0], swap_sem.at[i, 1], sibling)
+        swap.start()
+        gradient(low, rows_ref, grads, width, core)
+        items[mine8] = grads[:, :, lanes(width, core)]
+        share = far(grads, fin.at[tail8], swap_sem.at[i, 2], swap_sem.at[i, 3], sibling)
+        share.start()
+        keep = pltpu.make_async_copy(grads, fin.at[tail8], swap_sem.at[i, 4])
+        keep.start()
+        return swap, share, keep
+
+    def back_part():
+        own_ready(2)
+        fb_arrived()
+        wait_bytes(og, loc.at[4])
+        for j in range(NBLK):
+            choose(j, fac_b, own_rb, own_sb, kept_b, picked_b, dw)
+        project(0, fac_b, og)
+        scatter(0)
+
+    own_ready(0)
+    own_ready(1)
+    play(ORDER_OUT, fa, fb, P=back_part, R=lambda: reduce(0))
+    own_ready(3)
+    fa_arrived()
+    wait_bytes(hid, loc.at[5])
+    for j in range(NBLK):
+        choose(j, fac_a, own_ra, own_sa, kept_a, picked_a, hw)
+    project(1, fac_a, hid)
+    scatter(1)
+    gather(0, back_ref)
+    moves_a = hand_over(0, back_ref, hid, grads_a, items_a, fin_a, hw)
+    moves_a[0].wait_recv()
+    moves_b = []
+
+    def proj_part():
+        gather(1, proj_ref)
+        moves_b.extend(hand_over(1, proj_ref, og, grads_b, items_b, fin_b, dw))
+
+    play(ORDER_BACK, ra, rb, S=lambda: reduce(1), G=proj_part, X=lambda: moves_b[0].wait_recv())
+
+    ra_arrived()
+    rb_arrived()
+    for swap, share, keep in (moves_a, moves_b):
+        swap.wait_send()
+        share.wait()
+        keep.wait()
+    wait_bytes(idbuf.at[pl.ds(0, NDP - 1)], ids_sem.at[0])
+    for i in range(4):
+        wait_bytes(owns[i][1].at[pl.ds(0, OWNED)], sib.at[0, i])
+    for i in range(2):
+        wait_bytes(parts.at[i, pl.ds(0, NT - 1)], psum_sem.at[i, 0])
+        wait_bytes(sums.at[i, pl.ds(0, NT - 1)], psum_sem.at[i, 2])
+    fa_finish()
+    fb_finish()
+    ra_finish()
+    rb_finish()
+
+
+def last_kernel(table, fin_a, fin_b, fac, back, gh, ga, gb, acc_a, acc_b, buf_a, buf_b, ghb, gab, gbb, sems):
+    count = table[33, 0]
+
+    def arriving(p):
+        slot = table[32, p] >> 5
+        return (
+            pltpu.make_async_copy(fin_a.at[slot], buf_a.at[p], sems.at[0]),
+            pltpu.make_async_copy(fin_b.at[slot], buf_b.at[p], sems.at[4]),
+        )
+
+    def loop(step):
+        def run(p, carry):
+            step(p)
+            return carry
+
+        lax.fori_loop(0, count, run, 0)
+
+    def start(p):
+        for copy in arriving(p):
+            copy.start()
+
+    def wait(p):
+        for copy in arriving(p):
+            copy.wait()
+
+    loop(start)
+    for j in range(NBLK):
+        rows = pl.ds(j * BLOCK, BLOCK)
+        rows_out = adapter_scale * lax.dot_general(
+            back[j], fac[j], (((0,), (0,)), ((), ())), preferred_element_type=jnp.float32
+        )
+        ghb[rows] = rows_out.astype(jnp.bfloat16)
+        pltpu.make_async_copy(ghb.at[rows], gh.at[rows], sems.at[1]).start()
+    gab[...] = jnp.zeros_like(gab)
+    gbb[...] = jnp.zeros_like(gbb)
+    trio = ((acc_a, buf_a, gab), (acc_b, buf_b, gbb))
+
+    def clear(p):
+        for acc, _, _ in trio:
+            acc[table[32, p] & 31] = jnp.zeros(acc.shape[1:], jnp.float32)
+
+    def add(p):
+        for acc, buf, _ in trio:
+            acc[table[32, p] & 31] += buf[p].astype(jnp.float32)
+
+    def store(p):
+        for acc, _, out in trio:
+            out[table[32, p] & 31] = acc[table[32, p] & 31].astype(jnp.bfloat16)
+
+    loop(clear)
+    loop(wait)
+    loop(add)
+    loop(store)
+    ca = pltpu.make_async_copy(gab, ga, sems.at[2])
+    cb = pltpu.make_async_copy(gbb, gb, sems.at[3])
+    ca.start()
+    cb.start()
+    pltpu.make_async_copy(ghb, gh, sems.at[1]).wait()
+    ca.wait()
+    cb.wait()
+
+
+def shards(hidden, output_gradient, block_adapter_index, adapter_down_factors, adapter_up_factors):
+    rows, ff_local = hidden.shape
+    d_local = output_gradient.shape[1]
+    hw, dw = ff_local // 2, d_local // 2
+    bf16, f32 = jnp.bfloat16, jnp.float32
+    vmem = pl.BlockSpec(memory_space=pltpu.VMEM)
+    smem = pl.BlockSpec(memory_space=pltpu.SMEM)
+    anywhere = pl.BlockSpec(memory_space=pl.ANY)
+    dma = pltpu.SemaphoreType.DMA
+    rank = ADAPTER_RANK
+    streams = [
+        pltpu.VMEM((2, slots, rank, width), bf16) for slots in (SLOTS_OUT, SLOTS_BACK) for width in (hw, dw)
+    ]
+    scratch = [
+        pltpu.VMEM((NDP, 8, 128), jnp.int32),
+        pltpu.SMEM((40, 128), jnp.int32),
+        pltpu.VMEM((NBLK, rank, d_local), bf16),
+        pltpu.VMEM((NBLK, rank, BLOCK), bf16),
+        pltpu.VMEM((rows, ff_local), bf16),
+        pltpu.VMEM((rows, d_local), bf16),
+        pltpu.VMEM((NBLK, rank, ff_local), bf16),
+        pltpu.VMEM((NBLK, rank, d_local), bf16),
+        pltpu.VMEM((2 * OWNED, rank, hw), bf16),
+        pltpu.VMEM((2 * OWNED, rank, dw), bf16),
+        pltpu.VMEM((2 * OWNED, rank, hw), bf16),
+        pltpu.VMEM((2 * OWNED, rank, dw), bf16),
+        pltpu.VMEM((2 * SLOTS_OUT, rank, hw), bf16),
+        pltpu.VMEM((2 * SLOTS_OUT, rank, dw), bf16),
+        pltpu.VMEM((2 * NBLK, rank, hw), bf16),
+        pltpu.VMEM((2 * NBLK, rank, dw), bf16),
+        *streams,
+        *streams,
+        pltpu.VMEM((2 * SLOTS_BACK, rank, hw), bf16),
+        pltpu.VMEM((2 * SLOTS_BACK, rank, dw), bf16),
+        pltpu.VMEM((2, NT, 8, BLOCK), f32),
+        pltpu.VMEM((2, NT, 8, BLOCK), f32),
+        pltpu.VMEM((2, NT, 8, BLOCK), f32),
+        dma((7,)),
+        dma((2,)),
+        dma((2, 4)),
+        dma((2, 5)),
+        dma((4,)),
+        dma((4, 2, max(SLOTS_OUT, SLOTS_BACK))),
+        dma((4, 3)),
+        dma((2, 4)),
+    ]
+    table, fac, back, fin_a, fin_b = pl.pallas_call(
+        functools.partial(ring_kernel, hw, dw),
+        name="ring",
+        out_shape=(
+            jax.ShapeDtypeStruct((40, 128), jnp.int32),
+            jax.ShapeDtypeStruct((NBLK, rank, ff_local), bf16),
+            jax.ShapeDtypeStruct((NBLK, rank, BLOCK), bf16),
+            jax.ShapeDtypeStruct((NFIN, rank, ff_local), bf16),
+            jax.ShapeDtypeStruct((NFIN, rank, d_local), bf16),
+        ),
+        in_specs=[smem] + [anywhere] * 4,
+        out_specs=(vmem, vmem, vmem, anywhere, anywhere),
+        scratch_shapes=scratch,
+        compiler_params=pltpu.CompilerParams(
+            collective_id=0, has_side_effects=True, vmem_limit_bytes=VMEM_LIMIT
+        ),
+    )(block_adapter_index, hidden, output_gradient, adapter_down_factors, adapter_up_factors)
+
+    def finish(*_):
+        return pl.pallas_call(
+            last_kernel,
+            name="finish",
+            out_shape=(
+                jax.ShapeDtypeStruct((rows, ff_local), bf16),
+                jax.ShapeDtypeStruct(adapter_down_factors.shape, bf16),
+                jax.ShapeDtypeStruct(adapter_up_factors.shape, bf16),
+            ),
+            in_specs=[smem, anywhere, anywhere, vmem, vmem],
+            out_specs=(anywhere, anywhere, anywhere),
+            scratch_shapes=[
+                pltpu.VMEM((OWNED, rank, ff_local), f32),
+                pltpu.VMEM((OWNED, rank, d_local), f32),
+                pltpu.VMEM((NFIN, rank, ff_local), bf16),
+                pltpu.VMEM((NFIN, rank, d_local), bf16),
+                pltpu.VMEM((rows, ff_local), bf16),
+                pltpu.VMEM((OWNED, rank, ff_local), bf16),
+                pltpu.VMEM((OWNED, rank, d_local), bf16),
+                dma((5,)),
+            ],
+            compiler_params=pltpu.CompilerParams(vmem_limit_bytes=VMEM_LIMIT),
+        )(table, fin_a, fin_b, fac, back)
+
+    return lax.cond(
+        table[0, 8] > 0,
+        finish,
+        general,
+        hidden,
+        output_gradient,
+        block_adapter_index,
+        adapter_down_factors,
+        adapter_up_factors,
+    )
+
+
 def solution(mesh):
     placed = (
         P("dp", "tensor"),

time: 254 us -> 83.2 us (0.33)
  waiting for transfers between devices: 87.1 us -> 0 us
  Pallas kernels: 0 us -> 80.7 us
  blocking collectives: 76.1 us -> 0 us
  local copies, waits for them, and re-layouts: 34.7 us -> 0.6 us
  starting transfers between devices: 33.9 us -> 0 us
  matrix products: 18.9 us -> 0 us
    all_to_all x4 -> x0, waiting for transfers between devices: 87.1 us -> none  [the longest x1 39.2 us: shards(): lax.all_to_all(send_a, 'dp', split_axis=0, concat_axis=0, tiled=True)]
    pallas_call x0 -> x2, Pallas kernels: none -> 80.7 us  [the longest x1 76.3 us: shards(): pl.pallas_call(functools.partial(ring_kernel, hw, dw), name='ring', out_s...]
    psum x1 -> x0, blocking collectives: 61.4 us -> none  [shards(): proj, back = lax.psum((proj_part, back_part), 'tensor')]
    all_to_all x4 -> x0, starting transfers between devices: 33.9 us -> none  [the longest x1 18.8 us: shards(): lax.all_to_all(back_bb, 'dp', split_axis=0, concat_axis=0, tiled=True)]
    reshape x9 -> x0, local copies, waits for them, and re-layouts: 21.5 us -> none  [the longest x2 9.19 us: shards(): send_a = send_a.reshape(dp_size, CAP, ADAPTER_RANK, ff_local)]
    dot_general x11 -> x0, matrix products: 18.9 us -> none  [the longest x1 3.13 us: shards(): jnp.einsum('jtf,jrf->jtr', hid_blocks, down_factor, preferred_element_typ...]
    unnamed x1 -> x0, blocking collectives: 14.7 us -> none
    unnamed x9 -> x8, local copies, waits for them, and re-layouts: 5.59 us -> 0.02 us
  transfers between devices with their start and end apart: 4 -> 0, of which waited for: 4 -> 0; matrix products, arithmetic and copies ran while one was open for 13% -> 0% of each run, Pallas kernels for 0% -> 0%
where the time goes in v3:
time: 83.2 us; the launch traced here: 83.1 us
  Pallas kernels  80.7 us (97%)
  between operations  1.54 us (2%)
    pallas_call x1, Pallas kernels, shards(): pl.pallas_call(functools.partial(ring_kernel, hw, dw), name='ring', out_s...  76.3 us
    pallas_call x1, Pallas kernels, finish(): pl.pallas_call(last_kernel, name='finish', out_shape=(jax.ShapeDtypeStruc...  4.43 us

profile of v3, /device:TPU:1, one launch (start us, length us, event | category | flops | bytes accessed | tf_op | source)
XLA Modules:
  0.0 83.1 jit_solution(9988030849288161570)
XLA Ops:
  0.6 0.0 copy-start
  0.6 0.0 copy-start.1
  0.7 0.0 copy-start.2
  0.7 0.0 copy-start.3
  0.7 76.3 %ring.1 = (s32[40,128]{1,0:T(8,128)S(1)}, bf16[8,16,1792]{2,1,0:T(8,128)(2,1)}, bf16[8,16,128]{2,1,0:T(8,128)(2,1)S(1)}, bf16[68,16,1792]{2,1,0:T(8,128)(2,1)}, bf16[68,16,512]{2,1,0:T(8,128)(2,1)}) custom-call(s32[8]{0:T(128)} %ids_ref.1, bf16[1024,1792]{1,0:T(8,128)(2,1)} %hid_hbm.1, bf16[1024,512]{1,0:T(8,128)(2,1)} %og_hbm.1, ...), custom_call_target="tpu_custom_call" | custom-call | tf_op jit(solution)/shard_map/ring/pallas_call | solution.py:630
  76.9 0.6 slice.3
  78.2 0.0 copy-done
  78.2 0.0 copy-done.1
  78.2 0.0 copy-done.2
  78.2 0.0 copy-done.3
  78.2 4.7 %conditional.1 = ((bf16[1024,1792]{1,0:T(8,128)(2,1)}, bf16[32,16,1792]{2,1,0:T(8,128)(2,1)}, bf16[32,16,512]{2,1,0:T(8,128)(2,1)})) conditional(s32[]{:T(128)} %bitcast.19, (s32[8]{0:T(128)S(1)}, bf16[32,16,512]{2,1,0:T(8,128)(2,1)S(1)}, bf16[1024,512]{1,0:T(8,128)(2,1)S(1)}, bf16[32,16,1792]{2,1,0:T(8,128)(2,1)S(1)}, ...), branch_computations={%region_0.6_spmd, %region_5.7_spmd} | conditional | flops 387978816 | bytes 71245976 | solution.py:672
  78.4 4.4 %finish.1 = (bf16[1024,1792]{1,0:T(8,128)(2,1)}, bf16[32,16,1792]{2,1,0:T(8,128)(2,1)}, bf16[32,16,512]{2,1,0:T(8,128)(2,1)}) custom-call(s32[40,128]{1,0:T(8,128)S(1)} %get-tuple-element.26.table, bf16[68,16,1792]{2,1,0:T(8,128)(2,1)} %get-tuple-element.27.fin_a, bf16[68,16,512]{2,1,0:T(8,128)(2,1)} %get-tuple-element.28.fin_b, ...), custom_call_target="tpu_custom_call" | custom-call | tf_op jit(solution)/shard_map/cond/branch_1_fun/finish/pallas_call | solution.py:649
Async XLA Ops:
  0.6 77.5 %copy-start = (bf16[1024,512]{1,0:T(8,128)(2,1)S(1)}, bf16[1024,512]{1,0:T(8,128)(2,1)}, u32[]{:S(2)}) copy-start(bf16[1024,512]{1,0:T(8,128)(2,1)} %og_hbm.1) | copy-start | bytes 3145732
  0.6 77.5 %copy-start.1 = (bf16[32,16,1792]{2,1,0:T(8,128)(2,1)S(1)}, bf16[32,16,1792]{2,1,0:T(8,128)(2,1)}, u32[]{:S(2)}) copy-start(bf16[32,16,1792]{2,1,0:T(8,128)(2,1)} %a_hbm.1) | copy-start | bytes 5505028
  0.7 77.5 %copy-start.2 = (bf16[32,16,512]{2,1,0:T(8,128)(2,1)S(1)}, bf16[32,16,512]{2,1,0:T(8,128)(2,1)}, u32[]{:S(2)}) copy-start(bf16[32,16,512]{2,1,0:T(8,128)(2,1)} %b_hbm.1) | copy-start | bytes 1572868
  0.7 77.5 %copy-start.3 = (s32[8]{0:T(128)S(1)}, s32[8]{0:T(128)}, u32[]{:S(2)}) copy-start(s32[8]{0:T(128)} %ids_ref.1) | copy-start | bytes 100

commit v4 on v3

--- a/solution.py
+++ b/solution.py
@@ -19,9 +19,12 @@
 SLOTS_OUT = 25
 SLOTS_BACK = 26
 LAG = 6
-NFIN = 2 * SLOTS_BACK + 16
-ORDER_OUT = "bbbabbbababbababbababababaPaaaaRaa"
-ORDER_BACK = "aaSaaaaGXbabbababbababbababbababbab"
+TWO_FIRST, TWO = 8, 13
+ONE_FIRST, ONE = 3, 10
+EXPRESS = TWO + ONE
+NFIN = 2 * max(SLOTS_BACK, EXPRESS) + 16
+FLAG = 12
+ORDER = "baabaaabaPaaaaRaaaHaaaWAAQAAAASAAAAGAXBAAABAAB"
 VMEM_LIMIT = 56 * 1024 * 1024
 
 
@@ -182,21 +185,29 @@
     group = jnp.where(ahead > 0, src * 2 + jnp.where(minus, 1, 0), 16)
     order = group * 1024 + (4 - dist) * 128 + lane
     wide = tall(order)
+
+    def ranked(active):
+        column = jnp.transpose(tall(jnp.where(active, order, 32767)))
+        return over_all(jnp.where(jnp.logical_and((column >> 10) == (wide >> 10), column < wide), 1, 0))
+
+    everyone = lane >= 0
+    plain_rank = ranked(everyone)
     if shared is None:
-        active = lane >= 0
+        active, rank = everyone, plain_rank
     else:
         packed = tall(shared * 32768 + order)
         column = jnp.transpose(packed)
         same = (packed >> 10) == (column >> 10)
         active = over_all(jnp.where(jnp.logical_and(same, column < packed), 1, 0)) == 0
-    column = jnp.transpose(tall(jnp.where(active, order, 32767)))
-    rank = over_all(jnp.where(jnp.logical_and((column >> 10) == (wide >> 10), column < wide), 1, 0))
-    if shared is not None:
-        led = jnp.transpose(tall(jnp.where(active, rank, 0)))
+        led = jnp.transpose(tall(jnp.where(active, ranked(active), 0)))
         rank = over_all(jnp.where(same, led, 0))
-    result = []
+    hops = []
+    express = []
     longest = jnp.zeros((8, 128), jnp.int32)
+    crowded = jnp.zeros((8, 128), jnp.int32)
     for sign, act in ((1, plus), (-1, minus)):
+        age = (sign * (chip - src)) & 7
+        arrives = jnp.logical_and(act, age == dist)
         goes = jnp.logical_and(act, active)
         counts = [per_chip(jnp.logical_and(goes, dist > h)) for h in range(4)]
         starts = [jnp.zeros((8, 128), jnp.int32)]
@@ -210,7 +221,6 @@
         for h in range(4):
             here = turn(counts[h], sign * h)
             longest = jnp.maximum(longest, jnp.where(here > 0, starts[h] + here, 0))
-        age = (sign * (chip - src)) & 7
         out_start = jnp.zeros((8, 128), jnp.int32)
         in_start = jnp.zeros((8, 128), jnp.int32)
         before_chip = (chip - sign) & 7
@@ -218,12 +228,47 @@
             out_start = jnp.where(age == h, pick_row(starts[h], sub, chip), out_start)
             in_start = jnp.where(age == h + 1, pick_row(starts[h], sub, before_chip), in_start)
         leaves = jnp.logical_and(goes, age < dist)
-        arrives = jnp.logical_and(act, age == dist)
-        out_slot = out_start + rank
         in_slot = in_start + rank
         source = jnp.where(age == 0, own_index + 1, 65 + in_slot)
-        result.append((leaves, out_slot, source, arrives, in_slot))
-    return result, bcast(jnp.max(longest, axis=0, keepdims=True))
+        hops.append((leaves, out_start + rank, source, arrives, in_slot))
+
+        if shared is not None:
+            counts = [per_chip(jnp.logical_and(act, dist > h)) for h in range(4)]
+        single, third = counts[0] - counts[1], counts[2] - counts[3]
+        two_start = jnp.maximum(counts[1], TWO_FIRST)
+        one_start = jnp.maximum(single, ONE_FIRST)
+        passing4 = turn(counts[3], 2 * sign)
+        passing3 = turn(third, 2 * sign)
+        two_end = jnp.where(passing4 > 0, two_start + passing4, counts[1])
+        one_end = jnp.where(passing3 > 0, one_start + passing3, single)
+        full = jnp.logical_or(
+            jnp.logical_or(two_end > TWO, one_end > ONE), counts[2] > TWO_FIRST
+        )
+        crowded = jnp.maximum(crowded, jnp.where(full, 1, 0))
+        far_before = over_all(jnp.where(src == sub, counts[1], 0))
+        four_before = over_all(jnp.where(src == sub, counts[3], 0))
+        own = age == 0
+        passes = age == 2
+        as_two = jnp.logical_and(own, dist >= 2)
+        as_one = jnp.logical_and(own, dist == 1)
+        on_two = jnp.logical_and(passes, dist == 4)
+        on_one = jnp.logical_and(passes, dist == 3)
+        leaves = jnp.logical_and(
+            act, jnp.logical_or(jnp.logical_or(as_two, as_one), jnp.logical_or(on_two, on_one))
+        )
+        near_slot = TWO + plain_rank - far_before
+        third_slot = TWO + plain_rank - four_before
+        out_slot = jnp.where(as_one, near_slot, plain_rank)
+        out_slot = jnp.where(on_two, pick_row(two_start, sub, chip) + plain_rank, out_slot)
+        out_slot = jnp.where(on_one, pick_row(one_start, sub, chip) + third_slot, out_slot)
+        source = jnp.where(own, own_index + 1, 65 + plain_rank)
+        in_slot = jnp.where(dist == 1, near_slot, plain_rank)
+        in_slot = jnp.where(dist == 3, pick_row(one_start, sub, before_chip) + third_slot, in_slot)
+        in_slot = jnp.where(
+            dist == 4, pick_row(two_start, sub, (chip - 2 * sign) & 7) + plain_rank, in_slot
+        )
+        express.append((leaves, out_slot, source, arrives, in_slot))
+    return hops, express, bcast(jnp.max(longest, axis=0, keepdims=True)), over_all(crowded)
 
 
 def by_row(mask, place, value, rows):
@@ -241,44 +286,50 @@
     owner_chip = ids >> 6
     chip_slot = ids & 63
     mine = (ids >> 5) == me
-    fetch, longest_f = slot_plan(owner_chip, token_chip, chip_slot, ids, chip, sub, lane)
-    back, longest_b = slot_plan(token_chip, owner_chip, lane & 15, None, chip, sub, lane)
+    fetch, quick_fetch, longest_f, crowded_f = slot_plan(owner_chip, token_chip, chip_slot, ids, chip, sub, lane)
+    back, quick_back, longest_b, crowded_b = slot_plan(token_chip, owner_chip, lane & 15, None, chip, sub, lane)
     fits = jnp.logical_and(longest_f <= SLOTS_OUT, longest_b <= SLOTS_BACK)
-    columns = []
-    for plan in (fetch, back):
-        for leaves, out_slot, source, _, _ in plan:
-            columns.append(by_row(leaves, out_slot, source, 32))
-    where = jnp.where(owner_chip == token_chip, chip_slot + 1, 0)
-    for d in range(2):
-        where = jnp.where(fetch[d][3], 65 + d * SLOTS_OUT + fetch[d][4], where)
-    columns.append(by_row((lane >> 3) == me, lane & 7, where, 32))
+    fits = jnp.logical_and(fits, crowded_f + crowded_b == 0)
+    columns = {}
+    for at, plan in ((0, fetch), (2, back), (5, quick_fetch), (7, quick_back)):
+        for d, (leaves, out_slot, source, _, _) in enumerate(plan):
+            columns[at + d] = by_row(leaves, out_slot, source, 32)
+    for at, plan, slots in ((4, fetch, SLOTS_OUT), (9, quick_fetch, EXPRESS)):
+        where = jnp.where(owner_chip == token_chip, chip_slot + 1, 0)
+        for d in range(2):
+            where = jnp.where(plan[d][3], 65 + d * slots + plan[d][4], where)
+        columns[at] = by_row((lane >> 3) == me, lane & 7, where, 32)
     stays = jnp.logical_and(owner_chip == token_chip, token_chip == chip)
-    landing = jnp.where(stays, 2 * SLOTS_BACK + (lane & 15), -1)
-    for d in range(2):
-        landing = jnp.where(back[d][3], d * SLOTS_BACK + back[d][4], landing)
-    wanted = jnp.logical_and(landing >= 0, mine)
-    count = bcast(jnp.sum(jnp.where(wanted, 1, 0), axis=1, keepdims=True))
     line = lax.broadcasted_iota(jnp.int32, (128, 128), 1)
-    ahead = jnp.transpose(jnp.concatenate([jnp.where(wanted, lane, 128)] * 16, axis=0))
-    rank = bcast(jnp.sum(jnp.where(ahead < line, 1, 0), axis=0, keepdims=True))
-    entry = jnp.where(wanted, rank * 4096 + landing * 32 + (ids & 31), -1)
-    entry = jnp.transpose(jnp.concatenate([entry] * 16, axis=0))
-    listed = bcast(jnp.sum(jnp.where((entry >> 12) == line, entry & 4095, 0), axis=0, keepdims=True))
+    lists = []
+    for plan, slots in ((back, SLOTS_BACK), (quick_back, EXPRESS)):
+        landing = jnp.where(stays, 2 * slots + (lane & 15), -1)
+        for d in range(2):
+            landing = jnp.where(plan[d][3], d * slots + plan[d][4], landing)
+        if not lists:
+            wanted = jnp.logical_and(landing >= 0, mine)
+            count = bcast(jnp.sum(jnp.where(wanted, 1, 0), axis=1, keepdims=True))
+            ahead = jnp.transpose(tall(jnp.where(wanted, lane, 128)))
+            rank = bcast(jnp.sum(jnp.where(ahead < line, 1, 0), axis=0, keepdims=True))
+        entry = jnp.where(wanted, rank * 4096 + landing * 32 + (ids & 31), -1)
+        entry = jnp.transpose(tall(entry))
+        lists.append(bcast(jnp.sum(jnp.where((entry >> 12) == line, entry & 4095, 0), axis=0, keepdims=True)))
     wide_lane = lax.broadcasted_iota(jnp.int32, (32, 128), 1)
     table = jnp.concatenate([jnp.where(fits, 1, 0)] * 4, axis=0)
-    for i, column in enumerate(columns):
+    for i, column in columns.items():
         table = jnp.where(wide_lane == i, jnp.broadcast_to(column, (32, 128)), table)
-    return jnp.concatenate([table, jnp.where(sub == 0, listed, count)], axis=0)
+    last = jnp.where(sub == 0, lists[0], jnp.where(sub == 1, lists[1], count))
+    return jnp.concatenate([table, last], axis=0)
 
 
 def wait_bytes(ref, sem):
     pltpu.make_async_copy(ref, ref, sem).wait()
 
 
-def ring_kernel(hw, dw, ids_ref, hid_hbm, og_hbm, a_hbm, b_hbm, table_ref, fac_a, back_ref, fin_a, fin_b,
-                idbuf, table, fac_b, proj_ref, hid, og, grads_a, grads_b,
+def ring_kernel(hw, dw, ids_ref, hid_hbm, og_hbm, a_hbm, b_hbm, flag_ref, table_ref, fac_hbm, back_ref, fin_a, fin_b,
+                idbuf, table, fac_a, fac_b, proj_ref, hid, og, grads_a, grads_b,
                 own_ra, own_rb, own_sa, own_sb, picked_a, picked_b, items_a, items_b,
-                stage_fa, stage_fb, stage_ra, stage_rb, got_fa, got_fb, got_ra, got_rb, kept_a, kept_b,
+                stage_fa, stage_fb, stage_ra, stage_rb, got_fa, got_fb, got_ra, got_rb, kept_fa, kept_fb, kept_ra, kept_rb,
                 part, parts, sums, loc, ids_sem, sib, swap_sem, ring_send, ring_recv, fwd, psum_sem):
     me = lax.axis_index("dp")
     t = lax.axis_index("tensor")
@@ -337,85 +388,111 @@
     to_smem.start()
     to_smem.wait()
 
-    def stream(index, phase, own, stage, got, kept, land_at, keep_local, group):
+    def stream(index, column, own, stage, got, kept, land_at, keep_local, pieces, free):
         count = own.shape[0]
         slots = stage.shape[1]
-        behind = LAG // group
-        chunks = [(p, min(group, slots - p)) for p in range(0, slots, group)]
         everything = kept.at[pl.ds(0, 2 * slots)]
 
         def copy(d, q):
-            p, n = chunks[q]
+            p, n, hops = pieces[q]
             return far(
                 stage.at[d, pl.ds(p, n)],
                 got.at[d, pl.ds(p, n)],
                 ring_send.at[index],
                 ring_recv.at[index, d, q],
-                {"dp": lax.rem(chip + (1 if d == 0 else NCHIP - 1), NCHIP) * 2 + core},
+                {"dp": lax.rem(chip + (hops if d == 0 else NCHIP - hops), NCHIP) * 2 + core},
             )
 
         def landed(d, q):
             copy(d, q).wait_recv()
-            p, n = chunks[q]
+            p, n, _ = pieces[q]
             there = land_at(pl.ds(d * slots + p, n))
             far(got.at[d, pl.ds(p, n)], there, fwd.at[index, 1], fwd.at[index, 2], sibling).start()
             if keep_local:
                 pltpu.make_async_copy(got.at[d, pl.ds(p, n)], there, fwd.at[index, 0]).start()
             kept[pl.ds(d * slots + p, n)] = got[d, pl.ds(p, n)]
 
+        def send(d, q):
+            p, n, _ = pieces[q]
+            for i in range(n):
+                code = table[p + i, column + d]
+                value = own[jnp.clip(code - 1, 0, count - 1)]
+                if q >= free:
+                    passed = kept[d * slots + jnp.clip(code - 65, 0, slots - 1)]
+                    value = jnp.where(code > 64, passed, value)
+                stage[d, p + i] = value
+            copy(d, q).start()
+
+        def arrived():
+            if keep_local:
+                wait_bytes(everything, fwd.at[index, 0])
+            wait_bytes(everything, fwd.at[index, 2])
+
+        def finish():
+            wait_bytes(stage, ring_send.at[index])
+            wait_bytes(everything, fwd.at[index, 1])
+
+        return landed, send, arrived, finish
+
+    def hop_stream(index, column, own, stage, got, kept, land_at, keep_local):
+        slots = stage.shape[1]
+        pieces = [(p, min(2, slots - p), 1) for p in range(0, slots, 2)]
+        behind = LAG // 2
+        landed, send, arrived, finish = stream(
+            index, column, own, stage, got, kept, land_at, keep_local, pieces, behind
+        )
+
         def step(m):
             for d in range(2):
                 if m >= behind:
                     landed(d, m - behind)
-                if m < len(chunks):
-                    p, n = chunks[m]
-                    for i in range(n):
-                        code = table[p + i, phase * 2 + d]
-                        value = own[jnp.clip(code - 1, 0, count - 1)]
-                        if m >= behind:
-                            passed = kept[d * slots + jnp.clip(code - 65, 0, slots - 1)]
-                            value = jnp.where(code > 64, passed, value)
-                        stage[d, p + i] = value
-                    copy(d, m).start()
-
-        def arrived():
-            if keep_local:
-                wait_bytes(everything, fwd.at[index, 0])
-            wait_bytes(everything, fwd.at[index, 2])
-
-        def finish():
-            wait_bytes(stage, ring_send.at[index])
-            wait_bytes(everything, fwd.at[index, 1])
+                if m < len(pieces):
+                    send(d, m)
 
         return step, arrived, finish
 
-    def play(order, a, b, **others):
-        step = {"a": 0, "b": 0}
+    def express_stream(index, column, own, stage, got, kept, land_at, keep_local):
+        pieces = [(0, TWO_FIRST, 2), (TWO, ONE_FIRST, 1), (TWO_FIRST, TWO - TWO_FIRST, 2), (TWO + ONE_FIRST, ONE - ONE_FIRST, 1)]
+        landed, send, arrived, finish = stream(
+            index, column, own, stage, got, kept, land_at, keep_local, pieces, 2
+        )
+
+        def step(m):
+            for d in range(2):
+                for q in ((), (0,), (1, 2, 3))[m]:
+                    landed(d, q)
+                for q in ((0, 1), (2, 3), ())[m]:
+                    send(d, q)
+
+        return step, arrived, finish
+
+    def play(order, steps, others):
+        count = dict.fromkeys(steps, 0)
         for kind in order:
             if kind in others:
                 others[kind]()
             else:
-                (a if kind == "a" else b)(step[kind])
-                step[kind] += 1
-
-    fa, fa_arrived, fa_finish = stream(
-        0, 0, own_ra, stage_fa, got_fa, kept_a, lambda s: picked_a.at[s], False, 2
-    )
-    fb, fb_arrived, fb_finish = stream(
-        1, 0, own_rb, stage_fb, got_fb, kept_b, lambda s: picked_b.at[s], False, 2
-    )
-    ra, ra_arrived, ra_finish = stream(
-        2, 1, items_a, stage_ra, got_ra, kept_a, lambda s: fin_a.at[s, :, lanes(hw, core)], True, 2
-    )
-    rb, rb_arrived, rb_finish = stream(
-        3, 1, items_b, stage_rb, got_rb, kept_b, lambda s: fin_b.at[s, :, lanes(dw, core)], True, 2
-    )
-
-    def choose(j, fac, own_r, own_s, kept, picked, width):
-        code = table[j, 4]
+                steps[kind](count[kind])
+                count[kind] += 1
+
+    fa, fa_arrived, fa_finish = hop_stream(
+        0, 0, own_ra, stage_fa, got_fa, kept_fa, lambda s: picked_a.at[s], False
+    )
+    fb, fb_arrived, fb_finish = express_stream(
+        1, 5, own_rb, stage_fb, got_fb, kept_fb, lambda s: picked_b.at[s], False
+    )
+    ra, ra_arrived, ra_finish = hop_stream(
+        2, 2, items_a, stage_ra, got_ra, kept_ra, lambda s: fin_a.at[s, :, lanes(hw, core)], True
+    )
+    rb, rb_arrived, rb_finish = express_stream(
+        3, 7, items_b, stage_rb, got_rb, kept_rb, lambda s: fin_b.at[s, :, lanes(dw, core)], True
+    )
+
+    def choose(j, column, fac, own_r, own_s, kept, picked, width):
+        code = table[j, column]
         near = code <= 64
         at = jnp.clip(code - 1, 0, 2 * OWNED - 1)
-        away = jnp.clip(code - 65, 0, 2 * SLOTS_OUT - 1)
+        away = jnp.clip(code - 65, 0, picked.shape[0] - 1)
         fac[j, :, lanes(width, core)] = jnp.where(near, own_r[at], kept[away])
         fac[j, :, lanes(width, other)] = jnp.where(near, own_s[at], picked[away])
 
@@ -457,9 +534,8 @@
             )
             grads[j, :, lanes(width, which)] = grad.astype(jnp.bfloat16)
 
-    tail8 = pl.ds(2 * SLOTS_BACK + core * NBLK, NBLK)
-
-    def hand_over(i, low, rows_ref, grads, items, fin, width):
+    def hand_over(i, low, rows_ref, grads, items, fin, width, slots):
+        tail8 = pl.ds(2 * slots + core * NBLK, NBLK)
         gradient(low, rows_ref, grads, width, other)
         swap = far(cut(grads, width, other), items.at[mine8], swap_sem.at[i, 0], swap_sem.at[i, 1], sibling)
         swap.start()
@@ -476,33 +552,51 @@
         fb_arrived()
         wait_bytes(og, loc.at[4])
         for j in range(NBLK):
-            choose(j, fac_b, own_rb, own_sb, kept_b, picked_b, dw)
+            choose(j, 9, fac_b, own_rb, own_sb, kept_fb, picked_b, dw)
         project(0, fac_b, og)
         scatter(0)
 
+    def proj_part():
+        own_ready(3)
+        fa_arrived()
+        for j in range(NBLK):
+            choose(j, 4, fac_a, own_ra, own_sa, kept_fa, picked_a, hw)
+        project(1, fac_a, hid)
+        scatter(1)
+        pltpu.make_async_copy(fac_a, fac_hbm, loc.at[7]).start()
+
+    moves_a, moves_b = [], []
+
+    def give_a():
+        wait_bytes(hid, loc.at[5])
+        gather(0, back_ref)
+        moves_a.extend(hand_over(0, back_ref, hid, grads_a, items_a, fin_a, hw, SLOTS_BACK))
+
+    def give_b():
+        gather(1, proj_ref)
+        moves_b.extend(hand_over(1, proj_ref, og, grads_b, items_b, fin_b, dw, EXPRESS))
+
     own_ready(0)
     own_ready(1)
-    play(ORDER_OUT, fa, fb, P=back_part, R=lambda: reduce(0))
-    own_ready(3)
-    fa_arrived()
-    wait_bytes(hid, loc.at[5])
-    for j in range(NBLK):
-        choose(j, fac_a, own_ra, own_sa, kept_a, picked_a, hw)
-    project(1, fac_a, hid)
-    scatter(1)
-    gather(0, back_ref)
-    moves_a = hand_over(0, back_ref, hid, grads_a, items_a, fin_a, hw)
-    moves_a[0].wait_recv()
-    moves_b = []
-
-    def proj_part():
-        gather(1, proj_ref)
-        moves_b.extend(hand_over(1, proj_ref, og, grads_b, items_b, fin_b, dw))
-
-    play(ORDER_BACK, ra, rb, S=lambda: reduce(1), G=proj_part, X=lambda: moves_b[0].wait_recv())
-
+    play(
+        ORDER,
+        {"a": fa, "b": fb, "A": ra, "B": rb},
+        {
+            "P": back_part,
+            "R": lambda: reduce(0),
+            "H": give_a,
+            "W": lambda: moves_a[0].wait_recv(),
+            "Q": proj_part,
+            "S": lambda: reduce(1),
+            "G": give_b,
+            "X": lambda: moves_b[0].wait_recv(),
+        },
+    )
+
+    flag_ref[0] = table[0, FLAG]
     ra_arrived()
     rb_arrived()
+    wait_bytes(fac_a, loc.at[7])
     for swap, share, keep in (moves_a, moves_b):
         swap.wait_send()
         share.wait()
@@ -520,13 +614,12 @@
 
 
 def last_kernel(table, fin_a, fin_b, fac, back, gh, ga, gb, acc_a, acc_b, buf_a, buf_b, ghb, gab, gbb, sems):
-    count = table[33, 0]
+    count = table[34, 0]
 
     def arriving(p):
-        slot = table[32, p] >> 5
         return (
-            pltpu.make_async_copy(fin_a.at[slot], buf_a.at[p], sems.at[0]),
-            pltpu.make_async_copy(fin_b.at[slot], buf_b.at[p], sems.at[4]),
+            pltpu.make_async_copy(fin_a.at[table[32, p] >> 5], buf_a.at[p], sems.at[0]),
+            pltpu.make_async_copy(fin_b.at[table[33, p] >> 5], buf_b.at[p], sems.at[4]),
         )
 
     def loop(step):
@@ -592,11 +685,13 @@
     dma = pltpu.SemaphoreType.DMA
     rank = ADAPTER_RANK
     streams = [
-        pltpu.VMEM((2, slots, rank, width), bf16) for slots in (SLOTS_OUT, SLOTS_BACK) for width in (hw, dw)
+        pltpu.VMEM((2, slots, rank, width), bf16)
+        for slots, width in ((SLOTS_OUT, hw), (EXPRESS, dw), (SLOTS_BACK, hw), (EXPRESS, dw))
     ]
     scratch = [
         pltpu.VMEM((NDP, 8, 128), jnp.int32),
         pltpu.SMEM((40, 128), jnp.int32),
+        pltpu.VMEM((NBLK, rank, ff_local), bf16),
         pltpu.VMEM((NBLK, rank, d_local), bf16),
         pltpu.VMEM((NBLK, rank, BLOCK), bf16),
         pltpu.VMEM((rows, ff_local), bf16),
@@ -608,17 +703,19 @@
         pltpu.VMEM((2 * OWNED, rank, hw), bf16),
         pltpu.VMEM((2 * OWNED, rank, dw), bf16),
         pltpu.VMEM((2 * SLOTS_OUT, rank, hw), bf16),
-        pltpu.VMEM((2 * SLOTS_OUT, rank, dw), bf16),
+        pltpu.VMEM((2 * EXPRESS, rank, dw), bf16),
         pltpu.VMEM((2 * NBLK, rank, hw), bf16),
         pltpu.VMEM((2 * NBLK, rank, dw), bf16),
         *streams,
         *streams,
+        pltpu.VMEM((2 * SLOTS_OUT, rank, hw), bf16),
+        pltpu.VMEM((2 * EXPRESS, rank, dw), bf16),
         pltpu.VMEM((2 * SLOTS_BACK, rank, hw), bf16),
-        pltpu.VMEM((2 * SLOTS_BACK, rank, dw), bf16),
+        pltpu.VMEM((2 * EXPRESS, rank, dw), bf16),
         pltpu.VMEM((2, NT, 8, BLOCK), f32),
         pltpu.VMEM((2, NT, 8, BLOCK), f32),
         pltpu.VMEM((2, NT, 8, BLOCK), f32),
-        dma((7,)),
+        dma((8,)),
         dma((2,)),
         dma((2, 4)),
         dma((2, 5)),
@@ -627,10 +724,11 @@
         dma((4, 3)),
         dma((2, 4)),
     ]
-    table, fac, back, fin_a, fin_b = pl.pallas_call(
+    flag, table, fac, back, fin_a, fin_b = pl.pallas_call(
         functools.partial(ring_kernel, hw, dw),
         name="ring",
         out_shape=(
+            jax.ShapeDtypeStruct((1,), jnp.int32),
             jax.ShapeDtypeStruct((40, 128), jnp.int32),
             jax.ShapeDtypeStruct((NBLK, rank, ff_local), bf16),
             jax.ShapeDtypeStruct((NBLK, rank, BLOCK), bf16),
@@ -638,7 +736,7 @@
             jax.ShapeDtypeStruct((NFIN, rank, d_local), bf16),
         ),
         in_specs=[smem] + [anywhere] * 4,
-        out_specs=(vmem, vmem, vmem, anywhere, anywhere),
+        out_specs=(smem, vmem, anywhere, vmem, anywhere, anywhere),
         scratch_shapes=scratch,
         compiler_params=pltpu.CompilerParams(
             collective_id=0, has_side_effects=True, vmem_limit_bytes=VMEM_LIMIT
@@ -670,7 +768,7 @@
         )(table, fin_a, fin_b, fac, back)
 
     return lax.cond(
-        table[0, 8] > 0,
+        flag[0] > 0,
         finish,
         general,
         hidden,

time: 83.2 us -> 79.2 us (0.952)
  Pallas kernels: 80.7 us -> 77.5 us
    pallas_call x1, Pallas kernels: 76.3 us -> 73.1 us  [shards(): pl.pallas_call(functools.partial(ring_kernel, hw, dw), name='ring', out_s...]
where the time goes in v4:
time: 79.2 us
  Pallas kernels  77.5 us (98%)
  between operations  1.49 us (2%)
    pallas_call x1, Pallas kernels, shards(): pl.pallas_call(functools.partial(ring_kernel, hw, dw), name='ring', out_s...  73.1 us
    pallas_call x1, Pallas kernels, finish(): pl.pallas_call(last_kernel, name='finish', out_shape=(jax.ShapeDtypeStruc...  4.44 us

profile of v4, /device:TPU:1, one launch (start us, length us, event | category | flops | bytes accessed | tf_op | source)
XLA Modules:
  0.0 79.2 jit_solution(394720957959616279)
XLA Ops:
  0.6 0.0 copy-start
  0.6 0.0 copy-start.1
  0.7 0.0 copy-start.2
  0.7 0.0 copy-start.3
  0.7 73.1 %ring.1 = (s32[1]{0:T(128)}, s32[40,128]{1,0:T(8,128)S(1)}, bf16[8,16,1792]{2,1,0:T(8,128)(2,1)}, bf16[8,16,128]{2,1,0:T(8,128)(2,1)S(1)}, bf16[68,16,1792]{2,1,0:T(8,128)(2,1)}, /*index=5*/bf16[68,16,512]{2,1,0:T(8,128)(2,1)}) custom-call(s32[8]{0:T(128)} %ids_ref.1, bf16[1024,1792]{1,0:T(8,128)(2,1)} %hid_hbm.1, bf16[1024,512]{1,0:T(8,128)(2,1)} %og_hbm.1, ...), custom_call_target="tpu_custom_call" | custom-call | tf_op jit(solution)/shard_map/ring/pallas_call | solution.py:727
  74.3 0.0 copy-done
  74.4 0.0 copy-done.1
  74.4 0.0 copy-done.2
  74.4 0.0 copy-done.3
  74.4 4.7 %conditional.1 = ((bf16[1024,1792]{1,0:T(8,128)(2,1)}, bf16[32,16,1792]{2,1,0:T(8,128)(2,1)}, bf16[32,16,512]{2,1,0:T(8,128)(2,1)})) conditional(s32[]{:T(128)} %bitcast.19, (s32[8]{0:T(128)S(1)}, bf16[32,16,512]{2,1,0:T(8,128)(2,1)S(1)}, bf16[1024,512]{1,0:T(8,128)(2,1)S(1)}, bf16[32,16,1792]{2,1,0:T(8,128)(2,1)S(1)}, ...), branch_computations={%region_0.6_spmd, %region_5.7_spmd} | conditional | flops 387978816 | bytes 71245976 | solution.py:770
  74.6 4.4 %finish.1 = (bf16[1024,1792]{1,0:T(8,128)(2,1)}, bf16[32,16,1792]{2,1,0:T(8,128)(2,1)}, bf16[32,16,512]{2,1,0:T(8,128)(2,1)}) custom-call(s32[40,128]{1,0:T(8,128)S(1)} %get-tuple-element.26.table, bf16[68,16,1792]{2,1,0:T(8,128)(2,1)} %get-tuple-element.27.fin_a, bf16[68,16,512]{2,1,0:T(8,128)(2,1)} %get-tuple-element.28.fin_b, ...), custom_call_target="tpu_custom_call" | custom-call | tf_op jit(solution)/shard_map/cond/branch_1_fun/finish/pallas_call | solution.py:747
Async XLA Ops:
  0.6 73.7 %copy-start = (bf16[1024,512]{1,0:T(8,128)(2,1)S(1)}, bf16[1024,512]{1,0:T(8,128)(2,1)}, u32[]{:S(2)}) copy-start(bf16[1024,512]{1,0:T(8,128)(2,1)} %og_hbm.1) | copy-start | bytes 3145732
  0.6 73.7 %copy-start.1 = (bf16[32,16,1792]{2,1,0:T(8,128)(2,1)S(1)}, bf16[32,16,1792]{2,1,0:T(8,128)(2,1)}, u32[]{:S(2)}) copy-start(bf16[32,16,1792]{2,1,0:T(8,128)(2,1)} %a_hbm.1) | copy-start | bytes 5505028
  0.7 73.7 %copy-start.2 = (bf16[32,16,512]{2,1,0:T(8,128)(2,1)S(1)}, bf16[32,16,512]{2,1,0:T(8,128)(2,1)}, u32[]{:S(2)}) copy-start(bf16[32,16,512]{2,1,0:T(8,128)(2,1)} %b_hbm.1) | copy-start | bytes 1572868
  0.7 73.7 %copy-start.3 = (s32[8]{0:T(128)S(1)}, s32[8]{0:T(128)}, u32[]{:S(2)}) copy-start(s32[8]{0:T(128)} %ids_ref.1) | copy-start | bytes 100

commit v5 on v4

--- a/solution.py
+++ b/solution.py
@@ -326,8 +326,8 @@
     pltpu.make_async_copy(ref, ref, sem).wait()
 
 
-def ring_kernel(hw, dw, ids_ref, hid_hbm, og_hbm, a_hbm, b_hbm, flag_ref, table_ref, fac_hbm, back_ref, fin_a, fin_b,
-                idbuf, table, fac_a, fac_b, proj_ref, hid, og, grads_a, grads_b,
+def ring_kernel(hw, dw, ids_ref, hid_hbm, og_hbm, a_hbm, b_hbm, flag_ref, list_ref, fac_hbm, back_ref, fin_a, fin_b,
+                idbuf, table_ref, table, fac_a, fac_b, proj_ref, hid, og, grads_a, grads_b,
                 own_ra, own_rb, own_sa, own_sb, picked_a, picked_b, items_a, items_b,
                 stage_fa, stage_fb, stage_ra, stage_rb, got_fa, got_fb, got_ra, got_rb, kept_fa, kept_fb, kept_ra, kept_rb,
                 part, parts, sums, loc, ids_sem, sib, swap_sem, ring_send, ring_recv, fwd, psum_sem):
@@ -383,12 +383,14 @@
     ids = idbuf[0]
     for i in range(1, NDP):
         ids = ids + idbuf[i]
-    table_ref[...] = make_tables(ids, me)
+    tables = make_tables(ids, me)
+    table_ref[...] = tables
+    list_ref[...] = tables[32:]
     to_smem = pltpu.make_async_copy(table_ref, table, loc.at[6])
     to_smem.start()
     to_smem.wait()
 
-    def stream(index, column, own, stage, got, kept, land_at, keep_local, pieces, free):
+    def stream(index, column, own, stage, got, kept, land_at, keep_local, pieces, free, paired):
         count = own.shape[0]
         slots = stage.shape[1]
         everything = kept.at[pl.ds(0, 2 * slots)]
@@ -406,11 +408,15 @@
         def landed(d, q):
             copy(d, q).wait_recv()
             p, n, _ = pieces[q]
+            kept[pl.ds(d * slots + p, n)] = got[d, pl.ds(p, n)]
+            if paired and q % 2 == 0 and q + 1 < len(pieces):
+                return
+            if paired and q % 2:
+                p, n = p - pieces[q - 1][1], n + pieces[q - 1][1]
             there = land_at(pl.ds(d * slots + p, n))
             far(got.at[d, pl.ds(p, n)], there, fwd.at[index, 1], fwd.at[index, 2], sibling).start()
             if keep_local:
                 pltpu.make_async_copy(got.at[d, pl.ds(p, n)], there, fwd.at[index, 0]).start()
-            kept[pl.ds(d * slots + p, n)] = got[d, pl.ds(p, n)]
 
         def send(d, q):
             p, n, _ = pieces[q]
@@ -439,7 +445,7 @@
         pieces = [(p, min(2, slots - p), 1) for p in range(0, slots, 2)]
         behind = LAG // 2
         landed, send, arrived, finish = stream(
-            index, column, own, stage, got, kept, land_at, keep_local, pieces, behind
+            index, column, own, stage, got, kept, land_at, keep_local, pieces, behind, True
         )
 
         def step(m):
@@ -454,7 +460,7 @@
     def express_stream(index, column, own, stage, got, kept, land_at, keep_local):
         pieces = [(0, TWO_FIRST, 2), (TWO, ONE_FIRST, 1), (TWO_FIRST, TWO - TWO_FIRST, 2), (TWO + ONE_FIRST, ONE - ONE_FIRST, 1)]
         landed, send, arrived, finish = stream(
-            index, column, own, stage, got, kept, land_at, keep_local, pieces, 2
+            index, column, own, stage, got, kept, land_at, keep_local, pieces, 2, False
         )
 
         def step(m):
@@ -613,13 +619,13 @@
     rb_finish()
 
 
-def last_kernel(table, fin_a, fin_b, fac, back, gh, ga, gb, acc_a, acc_b, buf_a, buf_b, ghb, gab, gbb, sems):
-    count = table[34, 0]
+def last_kernel(lists, fin_a, fin_b, fac, back, gh, ga, gb, acc_a, acc_b, buf_a, buf_b, ghb, gab, gbb, sems):
+    count = lists[2, 0]
 
     def arriving(p):
         return (
-            pltpu.make_async_copy(fin_a.at[table[32, p] >> 5], buf_a.at[p], sems.at[0]),
-            pltpu.make_async_copy(fin_b.at[table[33, p] >> 5], buf_b.at[p], sems.at[4]),
+            pltpu.make_async_copy(fin_a.at[lists[0, p] >> 5], buf_a.at[p], sems.at[0]),
+            pltpu.make_async_copy(fin_b.at[lists[1, p] >> 5], buf_b.at[p], sems.at[4]),
         )
 
     def loop(step):
@@ -651,15 +657,15 @@
 
     def clear(p):
         for acc, _, _ in trio:
-            acc[table[32, p] & 31] = jnp.zeros(acc.shape[1:], jnp.float32)
+            acc[lists[0, p] & 31] = jnp.zeros(acc.shape[1:], jnp.float32)
 
     def add(p):
         for acc, buf, _ in trio:
-            acc[table[32, p] & 31] += buf[p].astype(jnp.float32)
+            acc[lists[0, p] & 31] += buf[p].astype(jnp.float32)
 
     def store(p):
         for acc, _, out in trio:
-            out[table[32, p] & 31] = acc[table[32, p] & 31].astype(jnp.bfloat16)
+            out[lists[0, p] & 31] = acc[lists[0, p] & 31].astype(jnp.bfloat16)
 
     loop(clear)
     loop(wait)
@@ -690,6 +696,7 @@
     ]
     scratch = [
         pltpu.VMEM((NDP, 8, 128), jnp.int32),
+        pltpu.VMEM((40, 128), jnp.int32),
         pltpu.SMEM((40, 128), jnp.int32),
         pltpu.VMEM((NBLK, rank, ff_local), bf16),
         pltpu.VMEM((NBLK, rank, d_local), bf16),
@@ -724,12 +731,12 @@
         dma((4, 3)),
         dma((2, 4)),
     ]
-    flag, table, fac, back, fin_a, fin_b = pl.pallas_call(
+    flag, lists, fac, back, fin_a, fin_b = pl.pallas_call(
         functools.partial(ring_kernel, hw, dw),
         name="ring",
         out_shape=(
             jax.ShapeDtypeStruct((1,), jnp.int32),
-            jax.ShapeDtypeStruct((40, 128), jnp.int32),
+            jax.ShapeDtypeStruct((8, 128), jnp.int32),
             jax.ShapeDtypeStruct((NBLK, rank, ff_local), bf16),
             jax.ShapeDtypeStruct((NBLK, rank, BLOCK), bf16),
             jax.ShapeDtypeStruct((NFIN, rank, ff_local), bf16),
@@ -765,7 +772,7 @@
                 dma((5,)),
             ],
             compiler_params=pltpu.CompilerParams(vmem_limit_bytes=VMEM_LIMIT),
-        )(table, fin_a, fin_b, fac, back)
+        )(lists, fin_a, fin_b, fac, back)
 
     return lax.cond(
         flag[0] > 0,

time: 79.2 us -> 79 us (level)
  no operation moved by 1% of the time
where the time goes in v5:
time: 79 us; the launch traced here: 78.9 us
  Pallas kernels  77.2 us (98%)
  between operations  1.49 us (2%)
    pallas_call x1, Pallas kernels, shards(): pl.pallas_call(functools.partial(ring_kernel, hw, dw), name='ring', out_s...  73 us
    pallas_call x1, Pallas kernels, finish(): pl.pallas_call(last_kernel, name='finish', out_shape=(jax.ShapeDtypeStruc...  4.18 us

profile of v5, /device:TPU:1, one launch (start us, length us, event | category | flops | bytes accessed | tf_op | source)
XLA Modules:
  0.0 78.9 jit_solution(14608597960719220195)
XLA Ops:
  0.6 0.0 copy-start
  0.6 0.0 copy-start.1
  0.7 0.0 copy-start.2
  0.7 0.0 copy-start.3
  0.7 73.0 %ring.1 = (s32[1]{0:T(128)}, s32[8,128]{1,0:T(8,128)S(1)}, bf16[8,16,1792]{2,1,0:T(8,128)(2,1)}, bf16[8,16,128]{2,1,0:T(8,128)(2,1)S(1)}, bf16[68,16,1792]{2,1,0:T(8,128)(2,1)}, /*index=5*/bf16[68,16,512]{2,1,0:T(8,128)(2,1)}) custom-call(s32[8]{0:T(128)} %ids_ref.1, bf16[1024,1792]{1,0:T(8,128)(2,1)} %hid_hbm.1, bf16[1024,512]{1,0:T(8,128)(2,1)} %og_hbm.1, ...), custom_call_target="tpu_custom_call" | custom-call | tf_op jit(solution)/shard_map/ring/pallas_call | solution.py:734
  74.3 0.0 copy-done
  74.3 0.0 copy-done.1
  74.3 0.0 copy-done.2
  74.3 0.0 copy-done.3
  74.3 4.4 %conditional.1 = ((bf16[1024,1792]{1,0:T(8,128)(2,1)}, bf16[32,16,1792]{2,1,0:T(8,128)(2,1)}, bf16[32,16,512]{2,1,0:T(8,128)(2,1)})) conditional(s32[]{:T(128)} %bitcast.19, (s32[8]{0:T(128)S(1)}, bf16[32,16,512]{2,1,0:T(8,128)(2,1)S(1)}, bf16[1024,512]{1,0:T(8,128)(2,1)S(1)}, bf16[32,16,1792]{2,1,0:T(8,128)(2,1)S(1)}, ...), branch_computations={%region_0.6_spmd, %region_5.7_spmd} | conditional | flops 387978816 | bytes 71245976 | solution.py:777
  74.5 4.2 %finish.1 = (bf16[1024,1792]{1,0:T(8,128)(2,1)}, bf16[32,16,1792]{2,1,0:T(8,128)(2,1)}, bf16[32,16,512]{2,1,0:T(8,128)(2,1)}) custom-call(s32[8,128]{1,0:T(8,128)S(1)} %get-tuple-element.26.lists, bf16[68,16,1792]{2,1,0:T(8,128)(2,1)} %get-tuple-element.27.fin_a, bf16[68,16,512]{2,1,0:T(8,128)(2,1)} %get-tuple-element.28.fin_b, ...), custom_call_target="tpu_custom_call" | custom-call | tf_op jit(solution)/shard_map/cond/branch_1_fun/finish/pallas_call | solution.py:754
Async XLA Ops:
  0.6 73.6 %copy-start = (bf16[1024,512]{1,0:T(8,128)(2,1)S(1)}, bf16[1024,512]{1,0:T(8,128)(2,1)}, u32[]{:S(2)}) copy-start(bf16[1024,512]{1,0:T(8,128)(2,1)} %og_hbm.1) | copy-start | bytes 3145732
  0.6 73.6 %copy-start.1 = (bf16[32,16,1792]{2,1,0:T(8,128)(2,1)S(1)}, bf16[32,16,1792]{2,1,0:T(8,128)(2,1)}, u32[]{:S(2)}) copy-start(bf16[32,16,1792]{2,1,0:T(8,128)(2,1)} %a_hbm.1) | copy-start | bytes 5505028
  0.7 73.6 %copy-start.2 = (bf16[32,16,512]{2,1,0:T(8,128)(2,1)S(1)}, bf16[32,16,512]{2,1,0:T(8,128)(2,1)}, u32[]{:S(2)}) copy-start(bf16[32,16,512]{2,1,0:T(8,128)(2,1)} %b_hbm.1) | copy-start | bytes 1572868
  0.7 73.6 %copy-start.3 = (s32[8]{0:T(128)S(1)}, s32[8]{0:T(128)}, u32[]{:S(2)}) copy-start(s32[8]{0:T(128)} %ids_ref.1) | copy-start | bytes 100
